TPU v7x, 32 devices: a whole 2x2x4 slice. The times are simulated.
32 devices in a mesh: wide: 8 (over y, x, core), narrow: 4 (over z).
Axes of the slice: x: 2, y: 2, z: 4, core: 2. Of those that a mesh axis runs over, the one named last changes fastest.
Arguments:
- tokens: bfloat16 [16384, 768], P('wide'), may hold values from -6 to 6
- cotangent: bfloat16 [16384, 768], P('wide'), may hold values from -6 to 6
- lengths: int32 [8, 4], P('wide'), may hold values from 0 to 2048, as said below
- query_weight: bfloat16 [768, 768], P(None, 'narrow'), may hold values from -0.21875 to 0.21875
- query_bias: bfloat16 [768], P('narrow'), may hold values from -2 to 2
- key_weight: bfloat16 [768, 768], P(None, 'narrow'), may hold values from -0.21875 to 0.21875
- key_bias: bfloat16 [768], P('narrow'), may hold values from -2 to 2
- value_weight: bfloat16 [768, 768], P(None, 'narrow'), may hold values from -0.21875 to 0.21875
- value_bias: bfloat16 [768], P('narrow'), may hold values from -2 to 2
- out_weight: bfloat16 [768, 768], P('narrow'), may hold values from -0.875 to 0.875
- out_bias: bfloat16 [768], replicated, may hold values from -2 to 2
- norm_gain: bfloat16 [768], replicated, may hold values from 0.5 to 1.5
- norm_shift: bfloat16 [768], replicated, may hold values from -2 to 2
- up_weight: bfloat16 [768, 3072], P(None, 'narrow'), may hold values from -0.21875 to 0.21875
- up_bias: bfloat16 [3072], P('narrow'), may hold values from -2 to 2
- down_weight: bfloat16 [3072, 768], P('narrow'), may hold values from -0.109375 to 0.109375
- down_bias: bfloat16 [768], replicated, may hold values from -2 to 2
- final_gain: bfloat16 [768], replicated, may hold values from 0.5 to 1.5
- final_shift: bfloat16 [768], replicated, may hold values from -2 to 2
Outputs:
- layer_out: bfloat16 [16384, 768], P('wide')
- tokens_grad: float32 [16384, 768], P('wide')
- queryweight_grad: float32 [768, 768], P(None, 'narrow')
- querybias_grad: float32 [768], P('narrow')
- keyweight_grad: float32 [768, 768], P(None, 'narrow')
- keybias_grad: float32 [768], P('narrow')
- valueweight_grad: float32 [768, 768], P(None, 'narrow')
- valuebias_grad: float32 [768], P('narrow')
- outweight_grad: float32 [768, 768], P('narrow')
- outbias_grad: float32 [768], replicated
- normgain_grad: float32 [768], replicated
- normshift_grad: float32 [768], replicated
- upweight_grad: float32 [768, 3072], P(None, 'narrow')
- upbias_grad: float32 [3072], P('narrow')
- downweight_grad: float32 [3072, 768], P('narrow')
- downbias_grad: float32 [768], replicated
- finalgain_grad: float32 [768], replicated
- finalshift_grad: float32 [768], replicated
Inputs may be any that keep to these rules, and one draw needn't show every extreme that they name: `lengths`: in each row the first few slots hold sequences of 64 tokens or more and the remaining slots are 0; a row sums to at most 2048; in every draw one row is a single sequence of 2048 tokens.
All inputs are finite; a program needn't handle non-finite values.
Results may differ from a plain program's by a relative error of at most 0.014.
Values sent between devices are 32-bit elements; how exact they have to be, the bound alone decides.
No kernel may reach another device: no remote copies, remote signals or barrier semaphores. Data moves between devices by JAX's collectives and lax.ppermute only.
A program may use at most 256 MiB of HBM per device.

v0:
```python
import math

import jax
import jax.numpy as jnp
from jax import lax
from jax.sharding import PartitionSpec as P

HEAD = 64


EPSILON = 1e-12
NEG_FILL = -1000000000.0


def layout(seq_lengths, count):
    token_place = jnp.arange(count, dtype=jnp.int32)
    seq_ends = jnp.cumsum(seq_lengths)
    seq_starts = seq_ends - seq_lengths
    segment = jnp.sum((token_place[:, None] >= seq_ends[None, :]).astype(jnp.int32), axis=1)
    slot_ids = jnp.arange(seq_lengths.shape[0], dtype=jnp.int32)
    first_place = jnp.sum(
        jnp.where(segment[:, None] == slot_ids[None, :], seq_starts[None, :], 0), axis=1
    )
    position = (token_place - first_place).astype(jnp.float32)
    live = (token_place < seq_ends[-1]).astype(jnp.float32)
    return (segment, position, live)


def turn_tables(position, head_size):
    frequency = jnp.exp(
        jnp.arange(head_size // 2, dtype=jnp.float32) * (-2.0 * math.log(10000.0) / head_size)
    )
    angles = position[:, None] * frequency[None, :]
    return (jnp.cos(angles)[:, None, :], jnp.sin(angles)[:, None, :])


def rotate(values, cosine, sine):
    pairs = values.reshape(values.shape[:-1] + (values.shape[-1] // 2, 2))
    even_part = pairs[..., 0]
    odd_part = pairs[..., 1]
    turned = jnp.stack(
        [even_part * cosine - odd_part * sine, even_part * sine + odd_part * cosine], axis=-1
    )
    return turned.reshape(values.shape)


def normalize(summed, gain, shift):
    centre = summed - jnp.mean(summed, axis=-1, keepdims=True)
    spread = jnp.mean(centre * centre, axis=-1, keepdims=True)
    return centre * lax.rsqrt(spread + EPSILON) * gain + shift


def exact_gelu(inner):
    return jax.nn.gelu(inner, approximate=False)


def body(
    tokens,
    cotangent,
    lengths,
    query_weight,
    query_bias,
    key_weight,
    key_bias,
    value_weight,
    value_bias,
    out_weight,
    out_bias,
    norm_gain,
    norm_shift,
    up_weight,
    up_bias,
    down_weight,
    down_bias,
    final_gain,
    final_shift,
):
    row_count = tokens.shape[0]
    local_heads = query_weight.shape[1] // HEAD
    local_width = local_heads * HEAD
    segment, position, live = layout(lengths[0], row_count)
    cosine, sine = turn_tables(position, HEAD)

    def project(weight, bias):
        return jnp.dot(tokens, weight, preferred_element_type=jnp.float32) + bias.astype(
            jnp.float32
        )

    query_pre = project(query_weight, query_bias).reshape(row_count, local_heads, HEAD)
    key_pre = project(key_weight, key_bias).reshape(row_count, local_heads, HEAD)
    query_low = rotate(query_pre, cosine, sine).astype(jnp.bfloat16)
    key_low = rotate(key_pre, cosine, sine).astype(jnp.bfloat16)
    value_low = (
        project(value_weight, value_bias).reshape(row_count, local_heads, HEAD).astype(jnp.bfloat16)
    )
    block_rows = min(512, row_count)
    block_count = row_count // block_rows

    def block_scores(query_block, segment_block):
        raw_scores = (
            jnp.einsum("qhd,khd->hqk", query_block, key_low, preferred_element_type=jnp.float32)
            * 0.125
        )
        same_seq = segment_block[:, None] == segment[None, :]
        return jnp.where(same_seq[None], raw_scores, NEG_FILL)

    attended_pieces = []
    lse_pieces = []
    for block_index in range(block_count):
        span = slice(block_index * block_rows, (block_index + 1) * block_rows)
        scores = block_scores(query_low[span], segment[span])
        row_peak = jnp.max(scores, axis=-1, keepdims=True)
        raised = jnp.exp(scores - row_peak)
        row_mass = jnp.sum(raised, axis=-1, keepdims=True)
        weights_low = (raised / row_mass).astype(jnp.bfloat16)
        attended_pieces.append(
            jnp.einsum("hqk,khd->qhd", weights_low, value_low, preferred_element_type=jnp.float32)
        )
        lse_pieces.append(row_peak + jnp.log(row_mass))
    attended_low = (
        jnp.concatenate(attended_pieces, axis=0)
        .reshape(row_count, local_width)
        .astype(jnp.bfloat16)
    )
    attn_total = lax.psum(
        jnp.dot(attended_low, out_weight, preferred_element_type=jnp.float32), "narrow"
    )
    summed_one = tokens.astype(jnp.float32) + attn_total + out_bias.astype(jnp.float32)
    hidden_one, norm_back = jax.vjp(
        normalize, summed_one, norm_gain.astype(jnp.float32), norm_shift.astype(jnp.float32)
    )
    hidden_low = hidden_one.astype(jnp.bfloat16)
    pre_act = jnp.dot(hidden_low, up_weight, preferred_element_type=jnp.float32) + up_bias.astype(
        jnp.float32
    )
    activated_low = exact_gelu(pre_act).astype(jnp.bfloat16)
    ffn_total = lax.psum(
        jnp.dot(activated_low, down_weight, preferred_element_type=jnp.float32), "narrow"
    )
    second = hidden_one + ffn_total + down_bias.astype(jnp.float32)
    final_value, final_back = jax.vjp(
        normalize, second, final_gain.astype(jnp.float32), final_shift.astype(jnp.float32)
    )
    layer_out = (final_value * live[:, None]).astype(jnp.bfloat16)
    second_grad, finalgain_grad, finalshift_grad = final_back(
        cotangent.astype(jnp.float32) * live[:, None]
    )
    downbias_grad = jnp.sum(second_grad, axis=0)
    second_low = second_grad.astype(jnp.bfloat16)
    downweight_grad = jnp.einsum(
        "tf,td->fd", activated_low, second_low, preferred_element_type=jnp.float32
    )
    act_grad = jnp.einsum("td,fd->tf", second_low, down_weight, preferred_element_type=jnp.float32)
    _, gelu_back = jax.vjp(exact_gelu, pre_act)
    (pre_grad,) = gelu_back(act_grad)
    upbias_grad = jnp.sum(pre_grad, axis=0)
    pre_low = pre_grad.astype(jnp.bfloat16)
    upweight_grad = jnp.einsum("td,tf->df", hidden_low, pre_low, preferred_element_type=jnp.float32)
    hidden_part = jnp.einsum("tf,df->td", pre_low, up_weight, preferred_element_type=jnp.float32)
    hidden_grad = second_grad + lax.psum(hidden_part, "narrow")
    summed_grad, normgain_grad, normshift_grad = norm_back(hidden_grad)
    outbias_grad = jnp.sum(summed_grad, axis=0)
    summed_low = summed_grad.astype(jnp.bfloat16)
    outweight_grad = jnp.einsum(
        "ta,td->ad", attended_low, summed_low, preferred_element_type=jnp.float32
    )
    attended_grad = jnp.einsum(
        "td,ad->ta", summed_low, out_weight, preferred_element_type=jnp.float32
    )
    attended_grad = attended_grad.astype(jnp.bfloat16).reshape(row_count, local_heads, HEAD)
    value_back = jnp.zeros((row_count, local_heads, HEAD), jnp.float32)
    key_grad = jnp.zeros((row_count, local_heads, HEAD), jnp.float32)
    query_pieces = []
    for block_index in range(block_count):
        span = slice(block_index * block_rows, (block_index + 1) * block_rows)
        query_block = query_low[span]
        scores = block_scores(query_block, segment[span])
        weights = jnp.exp(scores - lse_pieces[block_index])
        weights_low = weights.astype(jnp.bfloat16)
        grad_block = attended_grad[span]
        value_back = value_back + jnp.einsum(
            "hqk,qhd->khd", weights_low, grad_block, preferred_element_type=jnp.float32
        )
        weight_grad = jnp.einsum(
            "qhd,khd->hqk", grad_block, value_low, preferred_element_type=jnp.float32
        )
        row_inner = jnp.sum(weights * weight_grad, axis=-1, keepdims=True)
        score_low = (weights * (weight_grad - row_inner)).astype(jnp.bfloat16)
        query_pieces.append(
            jnp.einsum("hqk,khd->qhd", score_low, key_low, preferred_element_type=jnp.float32)
            * 0.125
        )
        key_grad = (
            key_grad
            + jnp.einsum("hqk,qhd->khd", score_low, query_block, preferred_element_type=jnp.float32)
            * 0.125
        )
    query_grad = jnp.concatenate(query_pieces, axis=0)
    _, turn_back = jax.vjp(lambda inner: rotate(inner, cosine, sine), query_pre)
    (query_back,) = turn_back(query_grad)
    (key_back,) = turn_back(key_grad)
    query_back = query_back.reshape(row_count, local_width)
    key_back = key_back.reshape(row_count, local_width)
    value_back = value_back.reshape(row_count, local_width)
    querybias_grad = jnp.sum(query_back, axis=0)
    keybias_grad = jnp.sum(key_back, axis=0)
    valuebias_grad = jnp.sum(value_back, axis=0)
    query_back_low = query_back.astype(jnp.bfloat16)
    key_back_low = key_back.astype(jnp.bfloat16)
    value_back_low = value_back.astype(jnp.bfloat16)
    queryweight_grad = jnp.einsum(
        "td,tc->dc", tokens, query_back_low, preferred_element_type=jnp.float32
    )
    keyweight_grad = jnp.einsum(
        "td,tc->dc", tokens, key_back_low, preferred_element_type=jnp.float32
    )
    valueweight_grad = jnp.einsum(
        "td,tc->dc", tokens, value_back_low, preferred_element_type=jnp.float32
    )
    token_part = jnp.einsum(
        "tc,dc->td", query_back_low, query_weight, preferred_element_type=jnp.float32
    )
    token_part = token_part + jnp.einsum(
        "tc,dc->td", key_back_low, key_weight, preferred_element_type=jnp.float32
    )
    token_part = token_part + jnp.einsum(
        "tc,dc->td", value_back_low, value_weight, preferred_element_type=jnp.float32
    )
    tokens_grad = summed_grad + lax.psum(token_part, "narrow")
    every_grad = lax.psum(
        (
            queryweight_grad,
            querybias_grad,
            keyweight_grad,
            keybias_grad,
            valueweight_grad,
            valuebias_grad,
            outweight_grad,
            outbias_grad,
            normgain_grad,
            normshift_grad,
            upweight_grad,
            upbias_grad,
            downweight_grad,
            downbias_grad,
            finalgain_grad,
            finalshift_grad,
        ),
        "wide",
    )
    return (
        layer_out,
        tokens_grad,
        every_grad[0],
        every_grad[1],
        every_grad[2],
        every_grad[3],
        every_grad[4],
        every_grad[5],
        every_grad[6],
        every_grad[7],
        every_grad[8],
        every_grad[9],
        every_grad[10],
        every_grad[11],
        every_grad[12],
        every_grad[13],
        every_grad[14],
        every_grad[15],
    )


def solution(mesh):
    in_specs = (
        P("wide", None),
        P("wide", None),
        P("wide", None),
        P(None, "narrow"),
        P("narrow"),
        P(None, "narrow"),
        P("narrow"),
        P(None, "narrow"),
        P("narrow"),
        P("narrow", None),
        P(),
        P(),
        P(),
        P(None, "narrow"),
        P("narrow"),
        P("narrow", None),
        P(),
        P(),
        P(),
    )
    out_specs = (
        P("wide", None),
        P("wide", None),
        P(None, "narrow"),
        P("narrow"),
        P(None, "narrow"),
        P("narrow"),
        P(None, "narrow"),
        P("narrow"),
        P("narrow", None),
        P(),
        P(),
        P(),
        P(None, "narrow"),
        P("narrow"),
        P("narrow", None),
        P(),
        P(),
        P(),
    )
    return jax.shard_map(body, mesh=mesh, in_specs=in_specs, out_specs=out_specs, check_vma=False)
```

profile of v0, /device:TPU:0, one launch (start us, length us, event | category | flops | bytes accessed | tf_op | source)
XLA Modules:
  0.0 1329.9 jit_solution(17165655381789309128)
XLA Ops:
  23.5 7.1 subtract_convert_fusion
  36.1 3.2 fusion.47
  39.3 3.9 broadcast_compare_fusion.3
  50.6 3.3 fusion.60
  61.1 3.1 fusion.63
  71.4 3.3 fusion.62
  81.8 3.1 fusion.61
  85.9 3.7 fusion.90
  89.9 225.6 %all-reduce.12.cloned.1.call-done = f32[2048,768]{1,0:T(8,128)} async-done(((f32[2048,768]{1,0:T(8,128)}), f32[2048,768]{1,0:T(8,128)}) %all-reduce.12.cloned.1.call-update) | async-done | bytes 6291472 | tf_op jit(solution)/shard_map/psum | solution.py:125
  315.4 4.6 fusion.79
  321.0 18.3 %multiply_convert_fusion.5 = (bf16[2048,768]{1,0:T(8,128)(2,1)S(1)}, f32[2048,768]{1,0:T(8,128)}, f32[2048,768]{1,0:T(8,128)}) fusion(f32[768]{0:T(1024)S(1)} %convert_element_type.162, bf16[768,768]{1,0:T(8,128)(2,1)S(1)} %copy-done, f32[2048,768]{1,0:T(8,128)S(1)} %get-tuple-element.50, f32[768]{0:T(1024)S(1)} %convert_element_type.160, ...), kind=kOutput, calls=%fused_computation.56 | convolution fusion | flops 2527592448 | bytes 23225344 | tf_op jit(solution)/shard_map/dot_general | solution.py:133
  340.9 4.5 fusion.91
  347.3 220.1 %all-reduce.14.cloned.1.call-done = f32[2048,768]{1,0:T(8,128)} async-done(((f32[2048,768]{1,0:T(8,128)}), f32[2048,768]{1,0:T(8,128)}) %all-reduce.14.cloned.1.call-update) | async-done | bytes 6291472 | tf_op jit(solution)/shard_map/psum | solution.py:137
  567.4 6.1 fusion.77
  575.4 3.6 multiply_reduce_fusion.4
  579.1 4.9 fusion.76
  584.0 9.3 fusion.87
  595.0 4.5 fusion.50
  600.3 221.2 %all-reduce.16.cloned.1.call-done = f32[2048,768]{1,0:T(8,128)} async-done(((f32[2048,768]{1,0:T(8,128)}), f32[2048,768]{1,0:T(8,128)}) %all-reduce.16.cloned.1.call-update) | async-done | bytes 6291472 | tf_op jit(solution)/shard_map/psum | solution.py:160
  821.5 8.9 multiply_reduce_fusion.5
  830.4 4.4 fusion.75
  834.8 3.2 copy-done.8
  839.5 3.2 multiply_reduce_fusion.3
  842.7 4.5 multiply_convert_fusion.3
  847.2 5.0 fusion.55
  852.2 5.3 fusion.93
  857.5 8.0 fusion.13
  865.5 6.8 multiply_reduce_fusion.2
  872.3 3.3 fusion.11
  875.6 6.6 multiply_reduce_fusion.1
  882.2 3.4 fusion.9
  885.6 6.3 multiply_reduce_fusion
  891.8 12.1 multiply_convert_fusion.2
  903.9 5.7 fusion.54
  909.6 3.8 convolution_add_fusion.5
  913.5 9.6 multiply_convert_fusion.1
  923.1 5.7 fusion.53
  931.5 6.3 multiply_convert_fusion
  947.4 5.9 multiply_add_fusion.3
  953.3 4.0 fusion.64
  961.3 7.0 fusion.80
  968.4 3.8 add_add_fusion.2
  972.8 8.2 fusion.72
  981.0 7.5 fusion.48
  995.7 198.4 %all-reduce.18.cloned.1.call-done = f32[2048,768]{1,0:T(8,128)} async-done(((f32[2048,768]{1,0:T(8,128)}), f32[2048,768]{1,0:T(8,128)}) %all-reduce.18.cloned.1.call-update) | async-done | bytes 6291472 | tf_op jit(solution)/shard_map/psum | solution.py:229
  1194.1 7.7 add_reduce_fusion
  1201.8 26.0 %all-reduce.4 = (f32[192]{0:T(256)}, f32[192]{0:T(256)}, f32[192]{0:T(256)}, f32[768]{0:T(1024)}, f32[768]{0:T(1024)}, /*index=5*/f32[768]{0:T(1024)}, f32[768]{...) all-reduce(f32[192]{0:T(256)S(1)} %reduce_sum.309, ...), channel_id=1, replica_groups=mesh['wide'=8,'narrow'=4] {'wide'}, use_global_device_ids=true, to_apply=%region_29.30 | all-reduce | flops 5952 | bytes 47616 | tf_op jit(solution)/shard_map/psum | solution.py:230
  1227.8 84.6 %all-reduce.20.cloned.1.call-done = (f32[768,192]{0,1:T(8,128)}, f32[768,192]{0,1:T(8,128)}, f32[768,192]{0,1:T(8,128)}, f32[192,768]{1,0:T(8,128)}, f32[768,768]{1,0:T(8,128)}, /*index=5*/f32[768,768]{1,0:T(8,128)}) async-done(((f32[768,192]{0,1:T(8,128)}, f32[768,192]{0,1:T(8,128)}, f32[768,192]{0,1:T(8,128)}, f32[192,768]{1,0:T(8,128)}, f32[768,768]{1,0:T(8,128)}, /*index=5*/f32[768,768]{1,0:T(8,128)}), ...) | async-done | bytes 7077904 | tf_op jit(solution)/shard_map/psum | solution.py:230
  (272 shorter events, 96.4 us)
Async XLA Ops:
  7.2 313.7 %copy-start = (bf16[768,768]{1,0:T(8,128)(2,1)S(1)}, bf16[768,768]{1,0:T(8,128)(2,1)}, u32[]{:S(2)}) copy-start(bf16[768,768]{1,0:T(8,128)(2,1)} %param.32) | copy-start | bytes 3538948
  7.2 10.2 copy-start.26
  7.2 308.2 %all-reduce.12.cloned.1.call-start = ((), (), s32[]{:S(2)}) async-start(), calls=%async_computation | async-start | bytes 12582912 | tf_op jit(solution)/shard_map/psum | solution.py:125
  23.5 7.2 copy-start.20
  23.5 7.2 copy-start.22
  35.8 10.1 copy-start.36
  35.9 38.8 %copy-start.34 = (bf16[512,3,64]{0,2,1:T(8,128)(2,1)}, bf16[512,3,64]{0,2,1:T(8,128)(2,1)S(1)}, u32[]{:S(2)}) copy-start(bf16[512,3,64]{0,2,1:T(8,128)(2,1)S(1)} %slice.93) | copy-start | bytes 589828
  36.0 17.9 %copy-start.30 = (bf16[512,3,64]{0,2,1:T(8,128)(2,1)}, bf16[512,3,64]{0,2,1:T(8,128)(2,1)S(1)}, u32[]{:S(2)}) copy-start(bf16[512,3,64]{0,2,1:T(8,128)(2,1)S(1)} %slice.99) | copy-start | bytes 589828
  36.1 28.1 %copy-start.32 = (bf16[512,3,64]{0,2,1:T(8,128)(2,1)}, bf16[512,3,64]{0,2,1:T(8,128)(2,1)S(1)}, u32[]{:S(2)}) copy-start(bf16[512,3,64]{0,2,1:T(8,128)(2,1)S(1)} %slice.96) | copy-start | bytes 589828
  89.7 477.7 %all-reduce.14.cloned.1.call-start = ((), (), s32[]{:S(2)}) async-start(), calls=%async_computation.1 | async-start | bytes 12582912 | tf_op jit(solution)/shard_map/psum | solution.py:137
  89.8 740.6 %copy-start.43 = (f32[768]{0:T(1024)}, f32[768]{0:T(1024)S(1)}, u32[]{:S(2)}) copy-start(f32[768]{0:T(1024)S(1)} %convert_element_type.159) | copy-start | bytes 9220
  89.8 477.6 %copy-start.53 = (f32[768]{0:T(1024)}, f32[768]{0:T(1024)S(1)}, u32[]{:S(2)}) copy-start(f32[768]{0:T(1024)S(1)} %convert_element_type.160) | copy-start | bytes 9220
  320.0 19.2 %copy-start.6 = (f32[2048,768]{1,0:T(8,128)}, f32[2048,768]{1,0:T(8,128)S(1)}, u32[]{:S(2)}) copy-start(f32[2048,768]{1,0:T(8,128)S(1)} %get-tuple-element.50) | copy-start | bytes 18874372
  320.9 509.5 %copy-start.39 = (f32[2048]{0:T(1024)}, f32[2048]{0:T(1024)S(1)}, u32[]{:S(2)}) copy-start(f32[2048]{0:T(1024)S(1)} %fusion.69) | copy-start | bytes 24580
  320.9 20.0 %copy-start.68 = (bf16[768,768]{1,0:T(8,128)(2,1)S(1)}, bf16[768,768]{1,0:T(8,128)(2,1)}, u32[]{:S(2)}) copy-start(bf16[768,768]{1,0:T(8,128)(2,1)} %param.34) | copy-start | bytes 3538948
  345.4 476.0 %all-reduce.16.cloned.1.call-start = ((), (), s32[]{:S(2)}) async-start(), calls=%async_computation.2 | async-start | bytes 12582912 | tf_op jit(solution)/shard_map/psum | solution.py:160
  575.4 8.5 slice-start.14
  583.9 9.4 copy-start.11
  583.9 237.5 %copy-start.49 = (f32[2048]{0:T(1024)}, f32[2048]{0:T(1024)S(1)}, u32[]{:S(2)}) copy-start(f32[2048]{0:T(1024)S(1)} %negate_multiply_fusion.2) | copy-start | bytes 24580
  599.5 594.6 %all-reduce.18.cloned.1.call-start = ((), (), s32[]{:S(2)}) async-start(), calls=%async_computation.3 | async-start | bytes 12582912 | tf_op jit(solution)/shard_map/psum | solution.py:229
  830.4 9.1 slice-start
  830.4 9.1 slice-start.1
  830.4 9.1 slice-start.2
  847.2 18.3 %slice-start.9 = ((s8[12582912]{0:T(1024)(128)(4,1)}), s8[4194304]{0:T(1024)(128)(4,1)S(1)}, s32[]{:S(2)}) async-start(s8[12582912]{0:T(1024)(128)(4,1)} %bitcast.140), calls=%async_computation.14 | async-start | bytes 8388608
  852.2 13.3 %slice-start.10 = ((s8[12582912]{0:T(1024)(128)(4,1)}), s8[4194304]{0:T(1024)(128)(4,1)S(1)}, s32[]{:S(2)}) async-start(s8[12582912]{0:T(1024)(128)(4,1)} %bitcast.140), calls=%async_computation.15 | async-start | bytes 8388608
  857.5 8.0 slice-start.11
  857.5 14.8 %slice-start.6 = ((s8[12582912]{0:T(1024)(128)(4,1)}), s8[4194304]{0:T(1024)(128)(4,1)S(1)}, s32[]{:S(2)}) async-start(s8[12582912]{0:T(1024)(128)(4,1)} %bitcast.138), calls=%async_computation.11 | async-start | bytes 8388608
  865.5 6.8 slice-start.7
  865.5 6.8 slice-start.8
  872.3 9.9 slice-start.3
  875.6 6.6 slice-start.5
  947.4 10.5 copy-start.25
  961.3 7.0 copy-start.38
  972.2 8.9 copy-start.40
  972.2 8.8 copy-start.44
  972.2 8.8 copy-start.54
  972.2 340.2 %all-reduce.20.cloned.1.call-start = ((), (), s32[]{:S(2)}) async-start(), calls=%async_computation.4 | async-start | bytes 14155776 | tf_op jit(solution)/shard_map/psum | solution.py:230
  972.8 8.2 copy-start.72
  981.0 7.5 copy-start.7
  995.6 206.1 %copy-start.51 = (f32[768]{0:T(1024)S(1)}, f32[768]{0:T(1024)}, u32[]{:S(2)}) copy-start(f32[768]{0:T(1024)} %get-tuple-element.20) | copy-start | bytes 9220
  995.7 206.1 %copy-start.52 = (f32[768]{0:T(1024)S(1)}, f32[768]{0:T(1024)}, u32[]{:S(2)}) copy-start(f32[768]{0:T(1024)} %get-tuple-element.23) | copy-start | bytes 9220
  995.7 206.1 %copy-start.55 = (f32[768]{0:T(1024)S(1)}, f32[768]{0:T(1024)}, u32[]{:S(2)}) copy-start(f32[768]{0:T(1024)} %get-tuple-element.18) | copy-start | bytes 9220
  995.7 206.1 %copy-start.56 = (f32[768]{0:T(1024)S(1)}, f32[768]{0:T(1024)}, u32[]{:S(2)}) copy-start(f32[768]{0:T(1024)} %get-tuple-element.22) | copy-start | bytes 9220
  995.7 206.1 %copy-start.57 = (f32[768]{0:T(1024)S(1)}, f32[768]{0:T(1024)}, u32[]{:S(2)}) copy-start(f32[768]{0:T(1024)} %get-tuple-element.52) | copy-start | bytes 9220
  995.7 206.1 %copy-start.58 = (f32[768]{0:T(1024)S(1)}, f32[768]{0:T(1024)}, u32[]{:S(2)}) copy-start(f32[768]{0:T(1024)} %get-tuple-element.109) | copy-start | bytes 9220
  1312.4 7.9 copy-start.19
  1312.4 9.3 copy-start.18
  1312.4 10.7 copy-start.1
  (46 other events, 162.0 us)
Sparse Core Ops, SparseCore 0:
  89.8 225.5 all-reduce.11
  345.6 221.8 all-reduce.13
  599.6 221.7 all-reduce.15
  972.3 221.7 all-reduce.17
  1199.2 113.1 all-reduce.19
where the time goes:
time: 1330 us
  waiting for transfers between devices  950 us (71%)
  matrix products  179 us (13%)
  other arithmetic  115 us (9%)
  local copies, waits for them, and re-layouts  44.3 us (3%)
  blocking collectives  26 us (2%)
  between operations  15.2 us (1%)
    psum x1, waiting for transfers between devices, body(): lax.psum(jnp.dot(attended_low, out_weight, preferred_element_type=jnp.flo...  226 us
    psum x1, waiting for transfers between devices, body(): hidden_grad = second_grad + lax.psum(hidden_part, 'narrow')  221 us
    psum x1, waiting for transfers between devices, body(): lax.psum(jnp.dot(activated_low, down_weight, preferred_element_type=jnp.f...  220 us
    psum x1, waiting for transfers between devices, body(): tokens_grad = summed_grad + lax.psum(token_part, 'narrow')  198 us
    psum x1, waiting for transfers between devices, body(): lax.psum((queryweight_grad, querybias_grad, keyweight_grad, keybias_grad,...  84.6 us
    unnamed x184, local copies, waits for them, and re-layouts  33.2 us
    convert_element_type x4, other arithmetic, body(): score_low = (weights * (weight_grad - row_inner)).astype(jnp.bfloat16)  32.5 us
  transfers between devices with their start and end apart: 5, of which 5 were waited for; matrix products, arithmetic and copies ran while one was open for 2% of the time, Pallas kernels for 0%

commit v1 on v0

v1 whole, which is shorter than its diff:
```python
import functools
import math

import jax
import jax.numpy as jnp
import numpy as np
from jax import lax
from jax.experimental import pallas as pl
from jax.experimental.pallas import tpu as pltpu
from jax.sharding import PartitionSpec as P

HEAD = 64
HALF = HEAD // 2
WIDE_ROWS = 128
EPSILON = 1e-12
LOG2E = 1.4426950408889634
MASK_FILL = -float(2**30)
SLOT_ROWS = 16
STRIP = 16
VMEM_LIMIT = 56 * 1024 * 1024
LAYER_VMEM_LIMIT = 60 * 1024 * 1024
F32 = jnp.float32
BF16 = jnp.bfloat16


def layout(seq_lengths, count):
    token_place = jnp.arange(count, dtype=jnp.int32)
    seq_ends = jnp.cumsum(seq_lengths)
    seq_starts = seq_ends - seq_lengths
    segment = jnp.sum((token_place[:, None] >= seq_ends[None, :]).astype(jnp.int32), axis=1)
    slot_ids = jnp.arange(seq_lengths.shape[0], dtype=jnp.int32)
    first_place = jnp.sum(
        jnp.where(segment[:, None] == slot_ids[None, :], seq_starts[None, :], 0), axis=1
    )
    position = (token_place - first_place).astype(F32)
    return (segment, position)


def normalize(summed, gain, shift):
    centre = summed - jnp.mean(summed, axis=-1, keepdims=True)
    spread = jnp.mean(centre * centre, axis=-1, keepdims=True)
    return centre * lax.rsqrt(spread + EPSILON) * gain + shift


def dot(left, right, left_dim, right_dim):
    return lax.dot_general(
        left, right, (((left_dim,), (right_dim,)), ((), ())), preferred_element_type=F32
    )


def by_strips(tall, work, *arrays):
    made = []
    for low in range(0, arrays[0].shape[0], tall):
        made.append(work(*[array[low : low + tall] for array in arrays]))
    return [jnp.concatenate(strips, axis=0) for strips in zip(*made)]


def fold_rows(values):
    total = values[:8]
    for low in range(8, values.shape[0], 8):
        total = total + values[low : low + 8]
    return total


def split_pairs(width):
    place = np.zeros((width, width), np.float32)
    for row in range(width):
        head, inner = divmod(row, HEAD)
        half, pair = divmod(inner, HALF)
        place[row, head * HEAD + 2 * pair + half] = 1.0
    return jnp.asarray(place, BF16)


ANY = pl.BlockSpec(memory_space=pl.ANY)


def prepare_kernel(
    place, turn, query_weight, key_weight, value_weight, bias_rows, packed, biases, piece, full
):
    width = turn.shape[0]
    made = 3 * width
    full[:width, :] = dot(turn[...], query_weight[...], 1, 0)
    full[width : 2 * width, :] = dot(turn[...], key_weight[...], 1, 0)
    full[2 * width : made, :] = value_weight[...].astype(F32)
    packed[0] = full[...].astype(BF16)
    biases[0] = jnp.zeros_like(biases[0])
    for index in range(3):
        row = jnp.broadcast_to(bias_rows[0:1, index * width : (index + 1) * width], (8, width))
        if index < 2:
            row = dot(row.astype(BF16), turn[...], 1, 1)
        biases[0, index : index + 1, :width] = row[:1]
    biases[0, 3:4, :] = bias_rows[1:2, :]
    if len(piece.shape) > 1:
        rows = piece.shape[0] - 8
        start = pl.multiple_of(place[0] * rows, 8)
        piece[:rows, :] = full[pl.ds(start, rows), :]
        piece[rows:, :] = biases[0]


def prepare(place, turn, query_weight, key_weight, value_weight, bias_rows, rows):
    width, dim = query_weight.shape
    total = 3 * width
    whole = lambda shape: pl.BlockSpec(shape, lambda i, place: (0,) * len(shape))
    piece = (rows + 8, dim) if rows else (8,)
    return pl.pallas_call(
        prepare_kernel,
        grid_spec=pltpu.PrefetchScalarGridSpec(
            num_scalar_prefetch=1,
            grid=(1,),
            in_specs=[whole((width, width))] + [whole((width, dim))] * 3 + [whole((8, dim))],
            out_specs=[
                whole((1, total, dim)),
                whole((1, 8, dim)),
                whole(piece),
            ],
            scratch_shapes=[pltpu.VMEM((total, dim), F32)],
        ),
        out_shape=[
            jax.ShapeDtypeStruct((1, total, dim), BF16),
            jax.ShapeDtypeStruct((1, 8, dim), F32),
            jax.ShapeDtypeStruct(piece, F32),
        ],
        compiler_params=pltpu.CompilerParams(vmem_limit_bytes=VMEM_LIMIT),
        name="prepare",
    )(place, turn, query_weight, key_weight, value_weight, bias_rows)


def cut_kernel(place, up, down, out, *refs):
    piece, full = refs[-2], refs[-1]
    rows = up.shape[0]
    piece[:rows, :] = up[...].astype(F32)
    piece[rows : 2 * rows, :] = down[...].astype(F32)
    few = piece.shape[0] - 2 * rows
    full[...] = out[...].astype(F32)
    piece[2 * rows :, :] = full[pl.ds(pl.multiple_of(place[0] * few, 8), few), :]


def cut_pieces(place, up, down, out, rows, few, after):
    dim = up.shape[1]
    here = lambda rows: pl.BlockSpec((rows, dim), lambda i, place: (place[0], 0))
    return pl.pallas_call(
        cut_kernel,
        grid_spec=pltpu.PrefetchScalarGridSpec(
            num_scalar_prefetch=1,
            grid=(1,),
            in_specs=[here(rows), here(rows), pl.BlockSpec(out.shape, lambda i, place: (0, 0))]
            + [ANY] * len(after),
            out_specs=pl.BlockSpec((2 * rows + few, dim), lambda i, place: (0, 0)),
            scratch_shapes=[pltpu.VMEM(out.shape, F32)],
        ),
        out_shape=jax.ShapeDtypeStruct((2 * rows + few, dim), F32),
        name="cut_pieces",
    )(place, up, down, out, *after)


def stack_kernel(count, *refs):
    pieces, mine, extra = refs[:count], refs[-2], refs[-1]
    rows = mine.shape[1]
    for index, piece in enumerate(pieces):
        mine[index] = piece[:rows, :]
        extra[index] = piece[rows:, :]


def stack_pieces(pieces, rows, after):
    tall, dim = pieces[0].shape
    count = len(pieces)
    vmem = pl.BlockSpec(memory_space=pltpu.VMEM)
    return pl.pallas_call(
        functools.partial(stack_kernel, count),
        in_specs=[vmem] * count + [ANY] * len(after),
        out_specs=[vmem, vmem],
        out_shape=[
            jax.ShapeDtypeStruct((count, rows, dim), F32),
            jax.ShapeDtypeStruct((count, tall - rows, dim), F32),
        ],
        compiler_params=pltpu.CompilerParams(vmem_limit_bytes=VMEM_LIMIT),
        name="stack_pieces",
    )(*pieces, *after)


def turn_kernel(own, gathered, *refs):
    refs[-1][...] = gathered[...]


def turn_pieces(own, gathered, after):
    shards, rows, dim = gathered.shape
    return pl.pallas_call(
        turn_kernel,
        grid_spec=pltpu.PrefetchScalarGridSpec(
            num_scalar_prefetch=1,
            grid=(shards - 1,),
            in_specs=[
                pl.BlockSpec((1, rows, dim), lambda j, own: ((own[0] + 1 + j) % shards, 0, 0))
            ]
            + [ANY] * len(after),
            out_specs=pl.BlockSpec((1, rows, dim), lambda j, own: (j, 0, 0)),
        ),
        out_shape=jax.ShapeDtypeStruct((shards - 1, rows, dim), F32),
        compiler_params=pltpu.CompilerParams(vmem_limit_bytes=VMEM_LIMIT),
        name="turn_pieces",
    )(own, gathered, *after)


def halve_kernel(side, ahead, *refs):
    upper, lower = refs[-2:]
    cut_row = upper.shape[1]
    upper[...] = side[:, :cut_row, :]
    lower[...] = ahead[:, cut_row:, :]


def halve_pieces(side, ahead, cut_row, after):
    count, rows, dim = side.shape
    vmem = pl.BlockSpec(memory_space=pltpu.VMEM)
    return pl.pallas_call(
        halve_kernel,
        in_specs=[vmem, vmem] + [ANY] * len(after),
        out_specs=[vmem, vmem],
        out_shape=[
            jax.ShapeDtypeStruct((count, cut_row, dim), F32),
            jax.ShapeDtypeStruct((count, rows - cut_row, dim), F32),
        ],
        compiler_params=pltpu.CompilerParams(vmem_limit_bytes=VMEM_LIMIT),
        name="halve_pieces",
    )(side, ahead, *after)


def join_kernel(upper, lower, *refs):
    joined = refs[-1]
    cut_row = upper.shape[1]
    joined[:, :cut_row, :] = upper[...]
    joined[:, cut_row:, :] = lower[...]


def join_pieces(upper, lower, after):
    count, cut_row, dim = upper.shape
    vmem = pl.BlockSpec(memory_space=pltpu.VMEM)
    return pl.pallas_call(
        join_kernel,
        in_specs=[vmem, vmem] + [ANY] * len(after),
        out_specs=vmem,
        out_shape=jax.ShapeDtypeStruct((count, cut_row + lower.shape[1], dim), F32),
        compiler_params=pltpu.CompilerParams(vmem_limit_bytes=VMEM_LIMIT),
        name="join_pieces",
    )(upper, lower, *after)


def start_copies(places, parts, begins, shard, first, size, target, sems):
    copies = []
    for index, (part, begin) in enumerate(zip(parts, begins)):
        low, high = max(first, begin), min(first + size, begin + part.shape[1])
        if low >= high:
            continue
        start = pl.multiple_of(places[index] * size + (low - first), 8)
        copy = pltpu.make_async_copy(
            part.at[shard, pl.ds(low - begin, high - low), :],
            target.at[pl.ds(start, high - low), :],
            sems.at[index],
        )
        copy.start()
        copies.append(copy)
    return copies


def project_kernel(begins, size, places, tokens, cosine, sine, slots, biases, *refs):
    count_parts = len(begins)
    query_t, key_n, key_t, value_t, value_n = refs[-8:-3] if count_parts else refs[-6:-1]
    heads = query_t.shape[0]
    width = heads * HEAD
    if count_parts:
        tokens_t = tokens[...]
    else:
        tokens_t = tokens[...].T
        refs[-1][...] = tokens_t
    count = tokens_t.shape[1]
    if count_parts:
        parts, packed = refs[:count_parts], refs[-3]
        stage, sems = refs[-2], refs[-1]

        @pl.when(pl.program_id(1) == 0)
        def _():
            shard = pl.program_id(0)
            for copy in start_copies(places, parts, begins, shard, 0, size, stage, sems):
                copy.wait()
            packed[0] = stage[...].astype(BF16)

    else:
        packed = refs[0]

    bias = biases[0].T[:width, :]
    bias = jnp.concatenate([bias[:, 0:1], bias[:, 1:2], bias[:, 2:3]], axis=0)
    made = dot(packed[0], tokens_t, 1, 0) + bias
    cos, sin = cosine[...], sine[...]
    same = slots[...]
    same_low = same.astype(BF16)
    row = lax.broadcasted_iota(jnp.int32, (HEAD, count), 0)
    mask_rows = (1.0 - same) * MASK_FILL
    key_mask = jnp.concatenate(
        [mask_rows, jnp.zeros((HEAD - SLOT_ROWS, count), F32)], axis=0
    ).astype(BF16)
    value_ones = jnp.where(row < 2, 1.0, 0.0).astype(BF16)
    row16 = lax.broadcasted_iota(jnp.int32, (16, count), 0)
    ones16 = jnp.where(row16 < 1, 1.0, 0.0).astype(BF16)

    def rotate(rows):
        even, odd = rows[:HALF], rows[HALF:]
        return jnp.concatenate([even * cos - odd * sin, even * sin + odd * cos], axis=0)

    for head in range(heads):
        low = head * HEAD
        query = rotate(made[low : low + HEAD]) * (0.125 * LOG2E)
        query_t[head, :HEAD, :] = query.astype(BF16)
        query_t[head, HEAD : HEAD + SLOT_ROWS, :] = same_low
        query_t[head, HEAD + SLOT_ROWS :, :] = jnp.zeros(
            (WIDE_ROWS - HEAD - SLOT_ROWS, count), BF16
        )
        key = rotate(made[width + low : width + low + HEAD]).astype(BF16)
        key_t[head] = key
        key_n[head] = jnp.concatenate([key, key_mask], axis=0).T
        value = made[2 * width + low : 2 * width + low + HEAD].astype(BF16)
        value_t[head, :HEAD, :] = value
        value_t[head, HEAD:, :] = ones16
        value_n[head] = jnp.concatenate([value, value_ones], axis=0).T


def project(places, parts, begins, size, packed, biases, tokens, cosine, sine, slots, heads, after):
    dim, count = tokens.shape if parts else tokens.shape[::-1]
    shards = biases.shape[0]
    block = min(1024, count)
    total = shards * heads
    token_block = pl.BlockSpec((dim, block), lambda j, i, ids: (0, i))
    rows = 3 * heads * HEAD
    shard_block = pl.BlockSpec((1, rows, dim), lambda j, i, ids: (j, 0, 0))
    spec = pltpu.PrefetchScalarGridSpec(
        num_scalar_prefetch=1,
        grid=(shards, count // block),
        in_specs=[
            token_block if parts else pl.BlockSpec((block, dim), lambda j, i, ids: (i, 0)),
            pl.BlockSpec((HALF, block), lambda j, i, ids: (0, i)),
            pl.BlockSpec((HALF, block), lambda j, i, ids: (0, i)),
            pl.BlockSpec((SLOT_ROWS, block), lambda j, i, ids: (0, i)),
            pl.BlockSpec((1, 8, dim), lambda j, i, ids: (j, 0, 0)),
        ]
        + ([ANY] * len(parts) if parts else [shard_block])
        + [ANY] * len(after),
        out_specs=[
            pl.BlockSpec((heads, WIDE_ROWS, block), lambda j, i, ids: (j, 0, i)),
            pl.BlockSpec((heads, block, WIDE_ROWS), lambda j, i, ids: (j, i, 0)),
            pl.BlockSpec((heads, HEAD, block), lambda j, i, ids: (j, 0, i)),
            pl.BlockSpec((heads, HEAD + 16, block), lambda j, i, ids: (j, 0, i)),
            pl.BlockSpec((heads, block, WIDE_ROWS), lambda j, i, ids: (j, i, 0)),
        ]
        + [shard_block if parts else token_block],
        scratch_shapes=[
            pltpu.VMEM((rows, dim), F32),
            pltpu.SemaphoreType.DMA((len(parts),)),
        ]
        if parts
        else [],
    )
    return pl.pallas_call(
        functools.partial(project_kernel, tuple(begins), size),
        grid_spec=spec,
        out_shape=[
            jax.ShapeDtypeStruct((total, WIDE_ROWS, count), BF16),
            jax.ShapeDtypeStruct((total, count, WIDE_ROWS), BF16),
            jax.ShapeDtypeStruct((total, HEAD, count), BF16),
            jax.ShapeDtypeStruct((total, HEAD + 16, count), BF16),
            jax.ShapeDtypeStruct((total, count, WIDE_ROWS), BF16),
        ]
        + [jax.ShapeDtypeStruct((shards, rows, dim) if parts else (dim, count), BF16)],
        compiler_params=pltpu.CompilerParams(vmem_limit_bytes=VMEM_LIMIT),
        name="project",
    )(places, tokens, cosine, sine, slots, biases, *(parts or [packed]), *after)


def attend_kernel(key_n, query_t, value_t, *refs):
    probs_t, out_low, out_full, inverse, even_scores, odd_scores, even_peak, odd_peak = refs[-8:]
    count = key_n.shape[1]
    width = query_t.shape[2]
    chunk = min(256, count)

    def run(new_scores, new_peak, scores, peak_ref):
        query = query_t[0]
        last_peak = jnp.broadcast_to(peak_ref[...], (STRIP, width))
        peak = None
        total = jnp.zeros((HEAD + 16, width), F32)
        for low in range(0, count, chunk):
            part = dot(key_n[0, low : low + chunk, :], query, 1, 0)
            raised = []
            for row in range(low, low + chunk, STRIP):
                strip = part[row - low : row - low + STRIP]
                new_scores[row : row + STRIP, :] = strip
                peak = strip if peak is None else jnp.maximum(peak, strip)
                strip = jnp.exp2(scores[row : row + STRIP, :] - last_peak).astype(BF16)
                probs_t[0, 0, row : row + STRIP, :] = strip
                raised.append(strip)
            raised = jnp.concatenate(raised, axis=0)
            total = total + dot(value_t[0, :, low : low + chunk], raised, 1, 0)
        new_peak[...] = jnp.max(peak, axis=0, keepdims=True)
        scale = 1.0 / total[HEAD : HEAD + 1, :]
        inverse[0] = scale
        out = total[:HEAD, :] * scale
        out_full[...] = out
        out_low[...] = out.astype(BF16)

    odd = lax.rem(pl.program_id(0), 2)

    @pl.when(odd == 0)
    def _():
        run(even_scores, even_peak, odd_scores, odd_peak)

    @pl.when(odd == 1)
    def _():
        run(odd_scores, odd_peak, even_scores, even_peak)


def attend(made, first, number, into, after):
    query_t, key_n, _, value_t, _ = made[:5]
    total, count, _ = key_n.shape
    width = min(1024, count)
    steps = count // width
    last = number * steps - 1
    now = lambda s: jnp.minimum(s, last)
    past = lambda s: jnp.maximum(s - 1, 0)
    head_now = lambda s: first + now(s) // steps
    head_past = lambda s: first + past(s) // steps
    into = list(into)
    return pl.pallas_call(
        attend_kernel,
        grid=(number * steps + 1,),
        in_specs=[
            pl.BlockSpec((1, count, WIDE_ROWS), lambda s: (head_now(s), 0, 0)),
            pl.BlockSpec((1, WIDE_ROWS, width), lambda s: (head_now(s), 0, now(s) % steps)),
            pl.BlockSpec((1, HEAD + 16, count), lambda s: (head_past(s), 0, 0)),
        ]
        + [ANY] * (len(into) + len(after)),
        out_specs=[
            pl.BlockSpec((1, 1, count, width), lambda s: (head_past(s), past(s) % steps, 0, 0)),
            pl.BlockSpec((HEAD, width), lambda s: (head_past(s), past(s) % steps)),
            pl.BlockSpec((HEAD, width), lambda s: (head_past(s), past(s) % steps)),
            pl.BlockSpec((1, 1, width), lambda s: (head_past(s), 0, past(s) % steps)),
        ],
        out_shape=[
            jax.ShapeDtypeStruct((total, steps, count, width), BF16),
            jax.ShapeDtypeStruct((total * HEAD, count), BF16),
            jax.ShapeDtypeStruct((total * HEAD, count), F32),
            jax.ShapeDtypeStruct((total, 1, count), F32),
        ],
        scratch_shapes=[
            pltpu.VMEM((count, width), F32),
            pltpu.VMEM((count, width), F32),
            pltpu.VMEM((1, width), F32),
            pltpu.VMEM((1, width), F32),
        ],
        input_output_aliases={3 + index: index for index in range(len(into))},
        compiler_params=pltpu.CompilerParams(vmem_limit_bytes=VMEM_LIMIT),
        name="attend",
    )(key_n, query_t, value_t, *into, *after)


def gelu_parts(inner):
    size = jnp.abs(inner)
    fall = jnp.exp2(inner * inner * (-0.5 * LOG2E))
    base = 1.0 + (0.3275911 * math.sqrt(0.5)) * size
    ratio = pl.reciprocal(base, approx=True)
    ratio = ratio * (2.0 - base * ratio)
    tail = 0.5 * 1.061405429 * ratio - 0.5 * 1.453152027
    tail = tail * ratio + 0.5 * 1.421413741
    tail = tail * ratio - 0.5 * 0.284496736
    tail = tail * ratio + 0.5 * 0.254829592
    tail = tail * ratio * fall
    share = jnp.where(inner < 0.0, tail, 1.0 - tail)
    density = fall * (1.0 / math.sqrt(2.0 * math.pi))
    return (inner * share).astype(BF16), (share + inner * density).astype(BF16)


def layer_kernel(
    groups,
    begins,
    sizes,
    places,
    ends,
    tokens,
    cotangent,
    vectors,
    biases_own,
    biases_rest,
    out_own,
    up_own,
    down_own,
    *refs,
):
    attended, refs = refs[: len(groups)], refs[len(groups) :]
    parts, refs = refs[: len(begins)], refs[len(begins) :]
    layer_out, summed_grad_ref, up_grad, down_grad, out_grad, small = refs[:6]
    attended_grads, refs = refs[6 : 6 + len(groups)], refs[6 + len(groups) :]
    (
        up_all,
        down_all,
        out_all,
        slopes,
        stage,
        up_sum,
        down_sum,
        sums,
        sems,
        out_sems,
    ) = refs
    step = pl.program_id(0)
    count, dim = tokens.shape
    shards = up_all.shape[0]
    width = out_own.shape[0]
    streams = 2
    rows = count // streams

    @pl.when(step == 0)
    def _():
        sums[...] = jnp.zeros_like(sums)
        up_sum[...] = jnp.zeros_like(up_sum)
        down_sum[...] = jnp.zeros_like(down_sum)
        out_grad[...] = jnp.zeros_like(out_grad)
        jobs = [
            (kind, target, shard)
            for shard in range(shards - 1)
            for kind, target in ((2, out_all), (0, up_all), (1, down_all))
        ]
        slots = stage.shape[0]

        def begin(number):
            kind, target, shard = jobs[number]
            slot = number % slots
            first = sum(sizes[:kind])
            return start_copies(
                places, parts, begins, shard, first, sizes[kind], stage.at[slot], sems.at[slot]
            )

        running = [begin(number) for number in range(slots)]
        up_all[0] = up_own[...]
        down_all[0] = down_own[...]
        out_all[0] = out_own[...]
        for number, (_, target, shard) in enumerate(jobs):
            for copy in running.pop(0):
                copy.wait()
            tall = target.shape[1]
            target[shard + 1] = stage[number % slots, :tall, :].astype(BF16)
            if number + slots < len(jobs):
                running.append(begin(number + slots))

    def mean(values):
        return jnp.sum(values, axis=-1, keepdims=True) * (1.0 / dim)

    out_bias, norm_gain, norm_shift = vectors[0:1, :], vectors[1:2, :], vectors[2:3, :]
    down_bias, final_gain, final_shift = vectors[3:4, :], vectors[4:5, :], vectors[5:6, :]
    hidden_biases = [biases_own[0, 3:4, :]]
    hidden_biases += [biases_rest[index, 3:4, :] for index in range(shards - 1)]
    where = [(group, part) for group, size in enumerate(groups) for part in range(size)]

    def fold(index, values):
        sums[index] += jnp.sum(values.reshape(rows // 8, 8, values.shape[1]), axis=0)

    def stream(low):
        here = slice(low, low + rows)
        total = tokens[here, :].astype(F32) + out_bias
        for shard, (group, part) in enumerate(where):
            seen = attended[group][part * width : (part + 1) * width, here]
            total = total + dot(seen, out_all[shard], 0, 0)
        yield
        centre = total - mean(total)
        norm_scale = lax.rsqrt(mean(centre * centre) + EPSILON)
        normal = centre * norm_scale
        hidden = normal * norm_gain + norm_shift
        hidden_low = hidden.astype(BF16)
        second = hidden + down_bias
        yield
        inner = dot(hidden_low, up_all[0], 1, 0) + hidden_biases[0]
        yield
        own_active = None
        for shard in range(shards):
            active, slope = gelu_parts(inner)
            slopes[shard, here, :] = slope
            if shard == 0:
                own_active = active
            yield
            if shard + 1 < shards:
                inner = dot(hidden_low, up_all[shard + 1], 1, 0) + hidden_biases[shard + 1]
            second = second + dot(active, down_all[shard], 1, 0)
            yield
        centre = second - mean(second)
        final_scale = lax.rsqrt(mean(centre * centre) + EPSILON)
        final = centre * final_scale
        token = step * count + low + lax.broadcasted_iota(jnp.int32, (rows, 1), 0)
        alive = jnp.where(token < ends[0], 1.0, 0.0)
        layer_out[here, :] = ((final * final_gain + final_shift) * alive).astype(BF16)
        grad = cotangent[here, :].astype(F32) * alive
        fold(2, grad * final)
        fold(3, grad)
        scaled = grad * final_gain
        second_grad = final_scale * (scaled - mean(scaled) - final * mean(scaled * final))
        fold(1, second_grad)
        second_low = second_grad.astype(BF16)
        yield
        hidden_grad = second_grad
        following = dot(second_low, down_all[0], 1, 1)
        down_sum[...] += dot(own_active, second_low, 0, 0)
        yield
        for shard in range(shards):
            inner_grad = following * slopes[shard, here, :].astype(F32)
            inner_low = inner_grad.astype(BF16)
            if shard == 0:
                fold(0, inner_grad)
            yield
            if shard + 1 < shards:
                following = dot(second_low, down_all[shard + 1], 1, 1)
            if shard == 0:
                up_sum[...] += dot(hidden_low, inner_low, 0, 0)
            hidden_grad = hidden_grad + dot(inner_low, up_all[shard], 1, 1)
            yield
        fold(4, hidden_grad * normal)
        fold(5, hidden_grad)
        scaled = hidden_grad * norm_gain
        summed_grad = norm_scale * (scaled - mean(scaled) - normal * mean(scaled * normal))
        fold(6, summed_grad)
        summed_grad_ref[here, :] = summed_grad
        summed_low = summed_grad.astype(BF16)
        yield
        out_grad[...] += dot(attended[0][:, here], summed_low, 1, 0)
        for shard, (group, part) in enumerate(where):
            attended_grads[group][part * width : (part + 1) * width, here] = dot(
                out_all[shard], summed_low, 1, 1
            )
        yield

    running = [stream(index * rows) for index in range(streams)]
    next(running[0])
    while running:
        for work in list(reversed(running)):
            try:
                next(work)
            except StopIteration:
                running.remove(work)

    @pl.when(step == pl.num_programs(0) - 1)
    def _():
        copies = [
            pltpu.make_async_copy(up_sum, up_grad, out_sems.at[0]),
            pltpu.make_async_copy(down_sum, down_grad, out_sems.at[1]),
        ]
        for copy in copies:
            copy.start()
        for index in range(7):
            small[index : index + 1, :] = jnp.sum(sums[index], axis=0, keepdims=True)
        small[7:8, :] = jnp.zeros((1, dim), F32)
        for copy in copies:
            copy.wait()


def layer(
    places,
    ends,
    attended,
    tokens,
    cotangent,
    vectors,
    biases,
    out_own,
    up_own,
    down_own,
    parts,
    begins,
    sizes,
):
    count, dim = tokens.shape
    width = out_own.shape[0]
    groups = tuple(seen.shape[0] // width for seen in attended)
    shards = sum(groups)
    hidden = up_own.shape[1]
    block = min(512, count)
    whole = lambda shape: pl.BlockSpec(shape, lambda i, *_: (0,) * len(shape))
    rowed = pl.BlockSpec((block, dim), lambda i, *_: (i, 0))
    columns = [pl.BlockSpec((size * width, block), lambda i, *_: (0, i)) for size in groups]
    far = pl.BlockSpec(memory_space=pltpu.HBM)
    spec = pltpu.PrefetchScalarGridSpec(
        num_scalar_prefetch=2,
        grid=(count // block,),
        in_specs=[rowed, rowed, whole((8, dim))]
        + [whole(bias.shape) for bias in biases]
        + [whole((width, dim)), whole((dim, hidden)), whole((hidden, dim))]
        + columns
        + [ANY] * len(parts),
        out_specs=[rowed, rowed, far, far, whole((width, dim)), whole((8, dim))] + columns,
        scratch_shapes=[
            pltpu.VMEM((shards, dim, hidden), BF16),
            pltpu.VMEM((shards, hidden, dim), BF16),
            pltpu.VMEM((shards, width, dim), BF16),
            pltpu.VMEM((shards, block, hidden), BF16),
            pltpu.VMEM((3, max(dim, hidden), dim), F32),
            pltpu.VMEM((dim, hidden), F32),
            pltpu.VMEM((hidden, dim), F32),
            pltpu.VMEM((7, 8, dim), F32),
            pltpu.SemaphoreType.DMA((3, len(parts))),
            pltpu.SemaphoreType.DMA((2,)),
        ],
    )
    return pl.pallas_call(
        functools.partial(layer_kernel, groups, tuple(begins), tuple(sizes)),
        grid_spec=spec,
        out_shape=[
            jax.ShapeDtypeStruct((count, dim), BF16),
            jax.ShapeDtypeStruct((count, dim), F32),
            jax.ShapeDtypeStruct((dim, hidden), F32),
            jax.ShapeDtypeStruct((hidden, dim), F32),
            jax.ShapeDtypeStruct((width, dim), F32),
            jax.ShapeDtypeStruct((8, dim), F32),
        ]
        + [jax.ShapeDtypeStruct(seen.shape, F32) for seen in attended],
        compiler_params=pltpu.CompilerParams(vmem_limit_bytes=LAYER_VMEM_LIMIT),
        name="layer",
    )(
        places,
        ends,
        tokens,
        cotangent,
        vectors,
        *biases,
        out_own,
        up_own,
        down_own,
        *attended,
        *parts,
    )


def own_grads_kernel(
    turn, back, tokens, out_grad, small, sums, query_grad, key_grad, value_grad, tail
):
    width, dim = out_grad.shape
    query_grad[...] = dot(dot(turn[...], back[0, 0], 0, 0).astype(BF16), tokens[...], 1, 0)
    key_grad[...] = dot(dot(turn[...], back[0, 1], 0, 0).astype(BF16), tokens[...], 1, 0)
    value_grad[...] = dot(back[0, 2], tokens[...], 1, 0)
    tail[:width, :] = out_grad[...]
    tail[width : width + 8, :] = small[...]
    tail[width + 8 :, :] = jnp.zeros((tail.shape[0] - width - 8, dim), F32)
    turned = turn[...].astype(F32)
    for index in range(3):
        row = jnp.sum(sums[0, index].T, axis=0, keepdims=True)
        if index < 2:
            row = lax.dot_general(
                jnp.broadcast_to(row, (8, width)),
                turned,
                (((1,), (0,)), ((), ())),
                precision=lax.Precision.HIGHEST,
                preferred_element_type=F32,
            )[:1]
        tail[width + 8 + index : width + 9 + index, :width] = row


def own_grads(turn, back, tokens, out_grad, small, sums):
    dim, width = tokens.shape[1], turn.shape[0]
    return pl.pallas_call(
        own_grads_kernel,
        out_shape=[jax.ShapeDtypeStruct((width, dim), F32)] * 3
        + [jax.ShapeDtypeStruct((width + 16, dim), F32)],
        compiler_params=pltpu.CompilerParams(vmem_limit_bytes=VMEM_LIMIT),
        name="own_grads",
    )(turn, back, tokens, out_grad, small, sums)


def tokens_kernel(groups, summed_grad, *refs):
    backs, packed, out = refs[: len(groups)], refs[len(groups) : -1], refs[-1]
    total = summed_grad[...]
    for back, weights, size in zip(backs, packed, groups):
        rows = weights.shape[1]
        for shard in range(size):
            total = total + dot(back[shard * rows : (shard + 1) * rows, :], weights[shard], 0, 0)
    out[...] = total


def tokens_back(summed_grad, backs, packed):
    count, dim = summed_grad.shape
    groups = tuple(weights.shape[0] for weights in packed)
    block = min(512, count)
    rowed = pl.BlockSpec((block, dim), lambda i: (i, 0))
    return pl.pallas_call(
        functools.partial(tokens_kernel, groups),
        grid=(count // block,),
        in_specs=[rowed]
        + [pl.BlockSpec((back.shape[0], block), lambda i: (0, i)) for back in backs]
        + [pl.BlockSpec(weights.shape, lambda i: (0, 0, 0)) for weights in packed],
        out_specs=rowed,
        out_shape=jax.ShapeDtypeStruct((count, dim), F32),
        compiler_params=pltpu.CompilerParams(vmem_limit_bytes=VMEM_LIMIT),
        name="tokens_back",
    )(summed_grad, *backs, *packed)


def attend_back_kernel(
    probs_t,
    value_n,
    key_t,
    query_t,
    out_full,
    out_grad,
    inverse,
    cosine,
    sine,
    back,
    sums,
    both_total,
):
    step = pl.program_id(1)
    count = value_n.shape[1]
    width = query_t.shape[2]
    chunk = min(256, count)

    @pl.when(step == 0)
    def _():
        both_total[...] = jnp.zeros_like(both_total)
        sums[...] = jnp.zeros_like(sums)

    grad = (out_grad[...] * inverse[0]).astype(BF16)
    inner = jnp.sum(grad.astype(F32) * out_full[...], axis=0, keepdims=True)
    inner_high = inner.astype(BF16)
    inner_low = (inner - inner_high.astype(F32)).astype(BF16)
    row = lax.broadcasted_iota(jnp.int32, (16, width), 0)
    tail = jnp.where(
        row == 0,
        -inner_high.astype(F32),
        jnp.where(row == 1, -inner_low.astype(F32), 0.0),
    ).astype(BF16)
    grad_wide = jnp.concatenate(
        [grad, tail, jnp.zeros((WIDE_ROWS - HEAD - 16, width), BF16)], axis=0
    )
    query = query_t[0, :HEAD, :]
    nothing = jnp.zeros((HEAD, width), BF16)
    grad_left = jnp.concatenate([grad, nothing], axis=0).T
    query_right = jnp.concatenate([nothing, query], axis=0).T
    query_total = jnp.zeros((HEAD, width), F32)
    changed = lambda low: dot(value_n[0, low : low + chunk, :], grad_wide, 1, 0)
    following = changed(0)
    for low in range(0, count, chunk):
        change = following
        if low + chunk < count:
            following = changed(low + chunk)
        weights = probs_t[0, 0, low : low + chunk, :]
        (score,) = by_strips(
            STRIP, lambda seen, other: ((seen.astype(F32) * other).astype(BF16),), weights, change
        )
        both_total[low : low + chunk, :] += dot(weights, grad_left, 1, 0) + dot(
            score, query_right, 1, 0
        )
        query_total = query_total + dot(key_t[0, :, low : low + chunk], score, 1, 0)

    def unrotate(rows, cos, sin):
        even, odd = rows[:HALF], rows[HALF:]
        return jnp.concatenate([even * cos + odd * sin, odd * cos - even * sin], axis=0)

    def fold(rows):
        total = rows[:, :128]
        for low in range(128, rows.shape[1], 128):
            total = total + rows[:, low : low + 128]
        return total

    here = pl.ds(pl.multiple_of(step * width, width), width)
    query_back = unrotate(query_total * 0.125, cosine[:, here], sine[:, here])
    back[0, 0, :, here] = query_back.astype(BF16)
    sums[0, 0] += fold(query_back)

    @pl.when(step == pl.num_programs(1) - 1)
    def _():
        both = both_total[...].T
        key_back = unrotate(both[HEAD:] * (1.0 / LOG2E), cosine[...], sine[...])
        back[0, 1] = key_back.astype(BF16)
        sums[0, 1] = fold(key_back)
        value_back = both[:HEAD]
        back[0, 2] = value_back.astype(BF16)
        sums[0, 2] = fold(value_back)


def attend_back(probs_t, value_n, key_t, query_t, out_full, out_grad, inverse, cosine, sine, heads):
    total, steps, count, width = probs_t.shape
    shards = total // heads
    place = lambda h, i: (h // heads, 0, h % heads, 0)
    return pl.pallas_call(
        attend_back_kernel,
        grid=(total, steps),
        in_specs=[
            pl.BlockSpec((1, 1, count, width), lambda h, i: (h, i, 0, 0)),
            pl.BlockSpec((1, count, WIDE_ROWS), lambda h, i: (h, 0, 0)),
            pl.BlockSpec((1, HEAD, count), lambda h, i: (h, 0, 0)),
            pl.BlockSpec((1, WIDE_ROWS, width), lambda h, i: (h, 0, i)),
            pl.BlockSpec((HEAD, width), lambda h, i: (h, i)),
            pl.BlockSpec((HEAD, width), lambda h, i: (h, i)),
            pl.BlockSpec((1, 1, width), lambda h, i: (h, 0, i)),
            pl.BlockSpec((HALF, count), lambda h, i: (0, 0)),
            pl.BlockSpec((HALF, count), lambda h, i: (0, 0)),
        ],
        out_specs=[
            pl.BlockSpec((1, 3, HEAD, count), place),
            pl.BlockSpec((1, 3, HEAD, 128), place),
        ],
        out_shape=[
            jax.ShapeDtypeStruct((shards, 3, heads * HEAD, count), BF16),
            jax.ShapeDtypeStruct((shards, 3, heads * HEAD, 128), F32),
        ],
        scratch_shapes=[pltpu.VMEM((count, 2 * HEAD), F32)],
        compiler_params=pltpu.CompilerParams(vmem_limit_bytes=VMEM_LIMIT),
        name="attend_back",
    )(probs_t, value_n, key_t, query_t, out_full, out_grad, inverse, cosine, sine)


def body(
    tokens,
    cotangent,
    lengths,
    query_weight,
    query_bias,
    key_weight,
    key_bias,
    value_weight,
    value_bias,
    out_weight,
    out_bias,
    norm_gain,
    norm_shift,
    up_weight,
    up_bias,
    down_weight,
    down_bias,
    final_gain,
    final_shift,
):
    count, dim = tokens.shape
    width = query_weight.shape[1]
    heads = width // HEAD
    narrow = lax.axis_size("narrow")
    wide = lax.axis_size("wide")
    place = lax.axis_index("wide")
    segment, position = layout(lengths[0], count)
    frequency = jnp.exp(
        jnp.arange(HALF, dtype=F32) * (-2.0 * math.log(10000.0) / HEAD)
    )
    angles = frequency[:, None] * position[None, :]
    cosine, sine = jnp.cos(angles), jnp.sin(angles)
    slots = (segment[None, :] == jnp.arange(SLOT_ROWS, dtype=jnp.int32)[:, None]).astype(F32)

    turn = split_pairs(width)
    empty = lambda number: jnp.zeros((number,), BF16)
    bias_rows = jnp.concatenate(
        [query_bias, key_bias, value_bias, empty(-3 * width % dim), up_bias, empty(6 * dim)]
    )
    bias_rows = bias_rows.astype(F32).reshape(8, dim)
    vectors = jnp.concatenate(
        [out_bias, norm_gain, norm_shift, down_bias, final_gain, final_shift, empty(2 * dim)]
    )
    vectors = vectors.astype(F32).reshape(8, dim)
    ends = jnp.sum(lengths[0]).astype(jnp.int32).reshape(1)
    permuted = wide == 8 and narrow == 4
    made = 3 * width
    slice_rows = made // wide if permuted else 0
    place_ref = place.astype(jnp.int32).reshape(1)
    packed_own, biases_own, attn_piece = prepare(
        place_ref, turn, query_weight.T, key_weight.T, value_weight.T, bias_rows, slice_rows
    )

    def shift(value, distance):
        moves = [((shard + distance) % narrow, shard) for shard in range(narrow)]
        return lax.ppermute(value, "narrow", moves)

    def flip(value, mask):
        return lax.ppermute(value, "wide", [(index, index ^ mask) for index in range(wide)])

    def gathered(block, distances):
        size = block.shape[0] // wide
        piece = lax.dynamic_slice_in_dim(block, place * size, size, axis=0).astype(F32)
        pieces = jnp.stack([shift(piece, distance) for distance in distances])
        return lax.all_gather(pieces, "wide", axis=1, tiled=True)

    def scattered(masks):
        return jnp.stack([place ^ mask for mask in masks]).astype(jnp.int32)

    nowhere = jnp.zeros((1,), jnp.int32)
    own = project(
        nowhere, [], (), 0, packed_own, biases_own, tokens, cosine, sine, slots, heads, []
    )
    own_seen = attend(own, 0, 1, [], [])
    masks = (0, 2, 4, 6, 6, 1, 3, 5, 7, 7)
    if permuted:
        sizes = (up_weight.shape[0] // wide, down_weight.shape[0] // wide, width // wide)
        cut_row = (slice_rows // 2 + 7) // 8 * 8
        mine, biases_rest = stack_pieces(
            [shift(attn_piece, distance) for distance in range(1, narrow)],
            slice_rows,
            [own_seen[3]],
        )
        side, ahead, core_mine = flip(mine, 2), flip(mine, 4), flip(mine, 1)
        layer_piece = cut_pieces(
            place_ref, up_weight, down_weight, out_weight, sizes[0], sizes[2], [mine]
        )
        layer_pieces = lax.all_gather(layer_piece, "narrow", axis=0)
        own_seen = attend(own, 1, heads - 1, own_seen, [layer_piece])
        upper, lower = halve_pieces(side, ahead, cut_row, [own_seen[3]])
        across = [flip(upper, 4), flip(lower, 2)]
        core = [core_mine, flip(side, 1), flip(ahead, 1)] + [flip(value, 1) for value in across]
        rest_parts = [mine, side, ahead] + across + core
        rest_begins = (0, 0, 0, 0, cut_row, 0, 0, 0, 0, cut_row)
        rest_places, rest_size = scattered(masks), slice_rows
    else:
        own_seen = attend(own, 1, heads - 1, own_seen, [])
        rest_parts = [gathered(packed_own[0], range(1, narrow))]
        biases_rest = jnp.stack([shift(biases_own[0], step) for step in range(1, narrow)])
        rest_begins, rest_places, rest_size = (0,), nowhere, made
    rest = project(
        rest_places, rest_parts, rest_begins, rest_size, None, biases_rest, own[5], cosine, sine,
        slots, heads, [own_seen[3]],
    )
    if permuted:
        narrow_ref = lax.axis_index("narrow").astype(jnp.int32).reshape(1)
        mine = turn_pieces(narrow_ref, layer_pieces, [rest[1]])
        side, ahead, core_mine = flip(mine, 2), flip(mine, 4), flip(mine, 1)
        rest_seen = attend(rest, 0, heads, [], [mine])
        rest_seen = attend(rest, heads, heads, rest_seen, [])
        cut_row = (sum(sizes) // 2 + 7) // 8 * 8
        upper, lower = halve_pieces(side, ahead, cut_row, [rest_seen[3]])
        across = [flip(upper, 4), flip(lower, 2)]
        rest_seen = attend(rest, 2 * heads, (narrow - 3) * heads, rest_seen, [upper])
        joined = join_pieces(*across, [rest_seen[3]])
        layer_parts = [mine, side, ahead, joined]
        layer_parts += [core_mine] + [flip(value, 1) for value in (side, ahead, joined)]
        layer_begins = (0,) * 8
        layer_places = scattered((0, 2, 4, 6, 1, 3, 5, 7))
    else:
        rest_seen = attend(rest, 0, (narrow - 1) * heads, [], [])
        blocks = [up_weight, down_weight, out_weight]
        sizes = tuple(block.shape[0] for block in blocks)
        layer_parts = [
            jnp.concatenate([gathered(block, range(1, narrow)) for block in blocks], axis=1)
        ]
        layer_begins, layer_places = (0,), nowhere
    (
        layer_out,
        summed_grad,
        upweight_grad,
        downweight_grad,
        outweight_grad,
        small,
        own_grad,
        rest_grad,
    ) = layer(
        layer_places,
        ends,
        [own_seen[1], rest_seen[1]],
        tokens,
        cotangent,
        vectors,
        [biases_own, biases_rest],
        out_weight,
        up_weight,
        down_weight,
        layer_parts,
        layer_begins,
        sizes,
    )

    def back(made_arrays, seen, grad):
        return attend_back(
            seen[0], made_arrays[4], made_arrays[2], made_arrays[0], seen[2], grad, seen[3],
            cosine, sine, heads,
        )

    own_back, own_sums = back(own, own_seen, own_grad)
    own_all = own_grads(turn, own_back, tokens, outweight_grad, small, own_sums)
    upweight_grad, downweight_grad, query_grad, key_grad, value_grad, tail = lax.psum(
        (upweight_grad, downweight_grad, *own_all), "wide"
    )
    small = tail[width:]
    rest_back, _ = back(rest, rest_seen, rest_grad)
    tokens_grad = tokens_back(
        summed_grad,
        [value.reshape(-1, count) for value in (own_back, rest_back)],
        [packed_own, rest[5]],
    )
    return (
        layer_out,
        tokens_grad,
        query_grad.T,
        small[8, :width],
        key_grad.T,
        small[9, :width],
        value_grad.T,
        small[10, :width],
        tail[:width],
        small[6],
        small[4],
        small[5],
        upweight_grad,
        small[0],
        downweight_grad,
        small[1],
        small[2],
        small[3],
    )


def solution(mesh):
    in_specs = (
        P("wide", None),
        P("wide", None),
        P("wide", None),
        P(None, "narrow"),
        P("narrow"),
        P(None, "narrow"),
        P("narrow"),
        P(None, "narrow"),
        P("narrow"),
        P("narrow", None),
        P(),
        P(),
        P(),
        P(None, "narrow"),
        P("narrow"),
        P("narrow", None),
        P(),
        P(),
        P(),
    )
    out_specs = (
        P("wide", None),
        P("wide", None),
        P(None, "narrow"),
        P("narrow"),
        P(None, "narrow"),
        P("narrow"),
        P(None, "narrow"),
        P("narrow"),
        P("narrow", None),
        P(),
        P(),
        P(),
        P(None, "narrow"),
        P("narrow"),
        P("narrow", None),
        P(),
        P(),
        P(),
    )
    return jax.shard_map(body, mesh=mesh, in_specs=in_specs, out_specs=out_specs, check_vma=False)
```

time: 1330 us -> 453 us (0.34)
  waiting for transfers between devices: 950 us -> 38.5 us
  Pallas kernels: 0 us -> 349 us
  matrix products: 179 us -> 0 us
  other arithmetic: 115 us -> 4.8 us
  blocking collectives: 26 us -> 0 us
  local copies, waits for them, and re-layouts: 44.3 us -> 23.4 us
  starting transfers between devices: 0.2 us -> 16.3 us
    psum x5 -> x1, waiting for transfers between devices: 950 us -> 15.6 us  [body(): lax.psum((upweight_grad, downweight_grad, *own_all), 'wide')]
    pallas_call x0 -> x19, Pallas kernels: none -> 349 us  [the longest x2 113 us: attend_back(): pl.pallas_call(attend_back_kernel, grid=(total, steps), in_specs=[pl.Bloc...]
    dot_general x42 -> x0, matrix products: 179 us -> none  [the longest x4 22.8 us: body(): jnp.einsum('qhd,khd->hqk', grad_block, value_low, preferred_element_type=...]
    reduce_sum x14 -> x0, other arithmetic: 53.4 us -> none  [the longest x4 19.9 us: normalize(): centre = summed - jnp.mean(summed, axis=-1, keepdims=True)]
    convert_element_type x16 -> x2, other arithmetic: 35.7 us -> 0.67 us  [the longest x1 0.67 us: body(): (segment[None, :] == jnp.arange(SLOT_ROWS, dtype=jnp.int32)[:, None]).ast...]
    psum x1 -> x0, blocking collectives: 26 us -> none  [body(): lax.psum((queryweight_grad, querybias_grad, keyweight_grad, keybias_grad,...]
    ppermute x0 -> x20, waiting for transfers between devices: none -> 22.8 us  [the longest x17 22.8 us: flip(): lax.ppermute(value, 'wide', [(index, index ^ mask) for index in range(wid...]
    unnamed x184 -> x59, local copies, waits for them, and re-layouts: 33.2 us -> 12.6 us
  transfers between devices with their start and end apart: 5 -> 22, of which waited for: 5 -> 10; matrix products, arithmetic and copies ran while one was open for 2% -> 2% of each run, Pallas kernels for 0% -> 47%
where the time goes in v1:
time: 453 us; the launch traced here: 447 us
  Pallas kernels  349 us (77%)
  waiting for transfers between devices  38.5 us (8%)
  local copies, waits for them, and re-layouts  23.4 us (5%)
  starting transfers between devices  16.3 us (4%)
  between operations  14.7 us (3%)
  other arithmetic  4.8 us (1%)
    pallas_call x2, Pallas kernels, attend_back(): pl.pallas_call(attend_back_kernel, grid=(total, steps), in_specs=[pl.Bloc...  113 us
    pallas_call x1, Pallas kernels, layer(): pl.pallas_call(functools.partial(layer_kernel, groups, tuple(begins), tup...  87.5 us
    pallas_call x5, Pallas kernels, attend(): pl.pallas_call(attend_kernel, grid=(number * steps + 1,), in_specs=[pl.Bl...  78.5 us
    pallas_call x2, Pallas kernels, project(): pl.pallas_call(functools.partial(project_kernel, tuple(begins), size), gr...  28.9 us
    ppermute x17, waiting for transfers between devices, flip(): lax.ppermute(value, 'wide', [(index, index ^ mask) for index in range(wid...  22.8 us
    pallas_call x1, Pallas kernels, tokens_back(): pl.pallas_call(functools.partial(tokens_kernel, groups), grid=(count // b...  16.2 us
    psum x1, waiting for transfers between devices, body(): lax.psum((upweight_grad, downweight_grad, *own_all), 'wide')  15.6 us
    unnamed x59, local copies, waits for them, and re-layouts  12.6 us
  transfers between devices with their start and end apart: 22, of which 10 were waited for; matrix products, arithmetic and copies ran while one was open for 2% of the time, Pallas kernels for 47%

profile of v1, /device:TPU:0, one launch (start us, length us, event | category | flops | bytes accessed | tf_op | source)
XLA Modules:
  0.0 447.0 jit_solution(5049757311796835921)
XLA Ops:
  7.3 2.8 concatenate.7
  10.7 2.6 prepare.1
  13.2 5.0 %collective-permute-start = (f32[80,768]{1,0:T(8,128)}, f32[80,768]{1,0:T(8,128)S(1)}, u32[]{:S(2)}, u32[]{:S(2)}) collective-permute-start(f32[80,768]{1,0:T(8,128)} %get-tuple-element.75), channel_id=1, source_target_pairs={{1,0},{2,1},{3,2},{0,3},{5,4},{6,5},{7,6},{4,7},{9,8},{10,9},{11,1... | collective-permute-start | bytes 737288 | tf_op jit(solution)/shard_map/ppermute | solution.py:967
  18.3 1.0 collective-permute-start.2
  19.3 0.8 reduce-window.4
  20.1 1.3 fusion.1
  21.6 1.8 multiply_sine_fusion
  24.1 7.0 %project.2 = (bf16[3,128,2048]{2,1,0:T(8,128)(2,1)}, bf16[3,2048,128]{2,1,0:T(8,128)(2,1)}, bf16[3,64,2048]{2,1,0:T(8,128)(2,1)}, bf16[3,80,2048]{2,1,0:T(8,128)...) custom-call(s32[1]{0:T(128)} %constant.14.clone.1.places, bf16[2048,768]{1,0:T(8,128)(2,1)} %tokens.5, ...), custom_call_target="tpu_custom_call" | custom-call | tf_op jit(solution)/shard_map/project/pallas_call | solution.py:360
  31.1 9.6 %attend.5 = (bf16[3,2,2048,1024]{3,2,1,0:T(8,128)(2,1)}, bf16[192,2048]{1,0:T(8,128)(2,1)}, f32[192,2048]{1,0:T(8,128)}, f32[3,1,2048]{2,1,0:T(1,128)}) custom-call(bf16[3,2048,128]{2,1,0:T(8,128)(2,1)} %get-tuple-element.77.key_n, bf16[3,128,2048]{2,1,0:T(8,128)(2,1)} %get-tuple-element.78.query_t, bf16[3,80,2048]{2,1,0:T(8,128)(2,1)} %get-tuple-element.79.value_t), custom_call_target="tpu_custom_call" | custom-call | tf_op jit(solution)/shard_map/attend/pallas_call | solution.py:428
  41.6 2.1 stack_pieces.1
  43.8 2.1 cut_pieces.1.refs_4_
  46.2 1.6 collective-permute-start.3
  47.8 1.5 collective-permute-start.4
  49.3 13.9 %attend.6 = (bf16[3,2,2048,1024]{3,2,1,0:T(8,128)(2,1)}, bf16[192,2048]{1,0:T(8,128)(2,1)}, f32[192,2048]{1,0:T(8,128)}, f32[3,1,2048]{2,1,0:T(1,128)}) custom-call(bf16[3,2048,128]{2,1,0:T(8,128)(2,1)} %get-tuple-element.77.key_n, ...), custom_call_target="tpu_custom_call", output_to_operand_aliasing={{0}: (3, {}), {1}: (4, {}), {2}: (5, {}), {3}: (6, {})} | custom-call | tf_op jit(solution)/shard_map/attend/pallas_call | solution.py:428
  64.2 2.2 halve_pieces.2
  66.4 1.4 collective-permute-start.5
  68.9 6.7 %collective-permute-done.5.refs_3_ = f32[3,40,768]{2,1,0:T(8,128)S(1)} collective-permute-done((f32[3,40,768]{2,1,0:T(8,128)}, f32[3,40,768]{2,1,0:T(8,128)S(1)}, u32[]{:S(2)}, u32[]{:S(2)}) %collective-permute-start.5) | collective-permute-done | bytes 368672 | tf_op jit(solution)/shard_map/ppermute | solution.py:970
  75.6 2.5 collective-permute-done.6.refs_4_
  78.7 1.3 collective-permute-done.11.refs_9_
  81.2 21.9 %project.3 = (bf16[9,128,2048]{2,1,0:T(8,128)(2,1)}, bf16[9,2048,128]{2,1,0:T(8,128)(2,1)}, bf16[9,64,2048]{2,1,0:T(8,128)(2,1)}, bf16[9,80,2048]{2,1,0:T(8,128)...) custom-call(s32[10]{0:T(128)} %stack.49.places, bf16[768,2048]{1,0:T(8,128)(2,1)} %get-tuple-element.87.tokens, ...), custom_call_target="tpu_custom_call" | custom-call | tf_op jit(solution)/shard_map/project/pallas_call | solution.py:360
  103.1 3.7 turn_pieces.1.refs_0_.refs_2_
  107.3 1.2 collective-permute-start.13
  108.5 18.1 %attend.7 = (bf16[9,2,2048,1024]{3,2,1,0:T(8,128)(2,1)}, bf16[576,2048]{1,0:T(8,128)(2,1)}, f32[576,2048]{1,0:T(8,128)}, f32[9,1,2048]{2,1,0:T(1,128)}) custom-call(bf16[9,2048,128]{2,1,0:T(8,128)(2,1)} %get-tuple-element.91.refs_0_.key_n, bf16[9,128,2048]{2,1,0:T(8,128)(2,1)} %get-tuple-element.92.query_t, bf16[9,80,2048]{2,1,0:T(8,128)(2,1)} %get-tuple-element.93.value_t, ...), custom_call_target="tpu_custom_call" | custom-call | tf_op jit(solution)/shard_map/attend/pallas_call | solution.py:428
  126.6 18.6 %attend.8 = (bf16[9,2,2048,1024]{3,2,1,0:T(8,128)(2,1)}, bf16[576,2048]{1,0:T(8,128)(2,1)}, f32[576,2048]{1,0:T(8,128)}, f32[9,1,2048]{2,1,0:T(1,128)}) custom-call(bf16[9,2048,128]{2,1,0:T(8,128)(2,1)} %get-tuple-element.91.refs_0_.key_n, ...), custom_call_target="tpu_custom_call", output_to_operand_aliasing={{0}: (3, {}), {1}: (4, {}), {2}: (5, {}), {3}: (6, {})} | custom-call | tf_op jit(solution)/shard_map/attend/pallas_call | solution.py:428
  145.2 7.3 %collective-permute-done.12.side.refs_3_ = f32[3,216,768]{2,1,0:T(8,128)} collective-permute-done((f32[3,216,768]{2,1,0:T(8,128)}, f32[3,216,768]{2,1,0:T(8,128)}, u32[]{:S(2)}, u32[]{:S(2)}) %collective-permute-start.12) | collective-permute-done | bytes 1990688 | tf_op jit(solution)/shard_map/ppermute | solution.py:970
  152.7 3.5 halve_pieces.3
  156.3 0.8 collective-permute-start.14
  157.1 1.3 collective-permute-start.15
  158.4 18.2 %attend.9 = (bf16[9,2,2048,1024]{3,2,1,0:T(8,128)(2,1)}, bf16[576,2048]{1,0:T(8,128)(2,1)}, f32[576,2048]{1,0:T(8,128)}, f32[9,1,2048]{2,1,0:T(1,128)}) custom-call(bf16[9,2048,128]{2,1,0:T(8,128)(2,1)} %get-tuple-element.91.refs_0_.key_n, ...), custom_call_target="tpu_custom_call", output_to_operand_aliasing={{0}: (3, {}), {1}: (4, {}), {2}: (5, {}), {3}: (6, {})} | custom-call | tf_op jit(solution)/shard_map/attend/pallas_call | solution.py:428
  177.3 1.7 collective-permute-done.15.lower
  179.0 1.3 collective-permute-done.14.upper
  180.3 1.0 copy-done.6
  181.2 3.0 join_pieces.1.refs_5_
  187.0 1.6 collective-permute-done.19.refs_9_
  188.6 87.5 %layer.1 = (bf16[2048,768]{1,0:T(8,128)(2,1)}, f32[2048,768]{1,0:T(8,128)}, f32[768,768]{1,0:T(8,128)}, f32[768,768]{1,0:T(8,128)}, f32[192,768]{1,0:T(8,128)}, ...) custom-call(s32[8]{0:T(128)} %stack.48.places, s32[1]{0:T(128)} %bitcast.8.ends, ...), custom_call_target="tpu_custom_call" | custom-call | tf_op jit(solution)/shard_map/layer/pallas_call | solution.py:704
  276.1 30.1 %attend_back.2 = (bf16[1,3,192,2048]{3,2,1,0:T(8,128)(2,1)}, f32[1,3,192,128]{3,2,1,0:T(8,128)}) custom-call(bf16[3,2,2048,1024]{3,2,1,0:T(8,128)(2,1)} %get-tuple-element.108.probs_t, bf16[3,2048,128]{2,1,0:T(8,128)(2,1)} %get-tuple-element.109.value_n, bf16[3,64,2048]{2,1,0:T(8,128)(2,1)} %get-tuple-element.110.key_t, ...), custom_call_target="tpu_custom_call" | custom-call | tf_op jit(solution)/shard_map/attend_back/pallas_call | solution.py:883
  306.2 6.3 %own_grads.1 = (f32[192,768]{1,0:T(8,128)}, f32[192,768]{1,0:T(8,128)}, f32[192,768]{1,0:T(8,128)}, f32[208,768]{1,0:T(8,128)}) custom-call(bf16[192,192]{1,0:T(8,128)(2,1)} %constant.38.clone.turn, bf16[1,3,192,2048]{3,2,1,0:T(8,128)(2,1)} %get-tuple-element.113.back, bf16[2048,768]{1,0:T(8,128)(2,1)} %tokens.5, f32[192,768]{1,0:T(8,128)} %get-tuple-element.121.out_grad, ...), custom_call_target="tpu_custom_call" | custom-call | tf_op jit(solution)/shard_map/own_grads/pallas_call | solution.py:759
  312.5 82.7 %attend_back.3 = (bf16[3,3,192,2048]{3,2,1,0:T(8,128)(2,1)}, f32[3,3,192,128]{3,2,1,0:T(8,128)}) custom-call(bf16[9,2,2048,1024]{3,2,1,0:T(8,128)(2,1)} %get-tuple-element.114.probs_t, bf16[9,2048,128]{2,1,0:T(8,128)(2,1)} %get-tuple-element.115.value_n, bf16[9,64,2048]{2,1,0:T(8,128)(2,1)} %get-tuple-element.116.key_t, ...), custom_call_target="tpu_custom_call" | custom-call | tf_op jit(solution)/shard_map/attend_back/pallas_call | solution.py:883
  395.2 16.2 %tokens_back.1 = f32[2048,768]{1,0:T(8,128)} custom-call(f32[2048,768]{1,0:T(8,128)} %get-tuple-element.107.summed_grad, bf16[576,2048]{1,0:T(8,128)(2,1)} %bitcast.30, bf16[1728,2048]{1,0:T(8,128)(2,1)} %bitcast.31, bf16[1,576,768]{2,1,0:T(8,128)(2,1)} %get-tuple-element.76.refs_0_.refs_2_, bf16[3,576,768]{2,1,0:T(8,128)(2,1)} %get-tuple-element.120.refs_3_), custom_call_target="tpu_custom_call" | custom-call | tf_op jit(solution)/shard_map/tokens_back/pallas_call | solution.py:783
  411.4 15.6 %all-reduce.3.cloned.1.call-done = (f32[768,192]{0,1:T(8,128)}, f32[208,768]{1,0:T(8,128)}, f32[768,192]{0,1:T(8,128)}, f32[768,192]{0,1:T(8,128)}, f32[768,768]{1,0:T(8,128)}, /*index=5*/f32[768,768]{1,0:T(8,128)}) async-done(((f32[768,192]{0,1:T(8,128)}, f32[208,768]{1,0:T(8,128)}, f32[768,192]{0,1:T(8,128)}, f32[768,192]{0,1:T(8,128)}, f32[768,768]{1,0:T(8,128)}, /*index=5*/f32[768,768]{1,0:T(8,128)}), ...) | async-done | bytes 7127056 | tf_op jit(solution)/shard_map/psum | solution.py:1072
  427.0 2.1 slice.58
  429.1 1.8 slice_reduce_fusion
  430.9 1.4 fusion.2
  432.3 1.9 copy.75
  435.0 0.8 copy.77
  435.8 1.4 copy.78
  437.2 1.1 copy-done.4
  438.3 1.4 copy.79
  (97 shorter events, 11.5 us)
Async XLA Ops:
  7.2 95.9 %all-gather.3.cloned.1.call-start = ((), (), s32[]{:S(2)}) async-start(), calls=%async_computation | async-start | bytes 3317760 | tf_op jit(solution)/shard_map/all_gather | solution.py:999
  13.2 27.5 %collective-permute-start = (f32[80,768]{1,0:T(8,128)}, f32[80,768]{1,0:T(8,128)S(1)}, u32[]{:S(2)}, u32[]{:S(2)}) collective-permute-start(f32[80,768]{1,0:T(8,128)} %get-tuple-element.75), channel_id=1, source_target_pairs={{1,0},{2,1},{3,2},{0,3},{5,4},{6,5},{7,6},{4,7},{9,8},{10,9},{11,1... | collective-permute-start | bytes 737288 | tf_op jit(solution)/shard_map/ppermute | solution.py:967
  18.3 22.5 %collective-permute-start.1 = (f32[80,768]{1,0:T(8,128)}, f32[80,768]{1,0:T(8,128)S(1)}, u32[]{:S(2)}, u32[]{:S(2)}) collective-permute-start(f32[80,768]{1,0:T(8,128)} %get-tuple-element.75), channel_id=1, source_target_pairs={{2,0},{3,1},{0,2},{1,3},{6,4},{7,5},{4,6},{5,7},{10,8},{11,9},{8,1... | collective-permute-start | bytes 737288 | tf_op jit(solution)/shard_map/ppermute | solution.py:967
  18.3 22.5 %collective-permute-start.2 = (f32[80,768]{1,0:T(8,128)}, f32[80,768]{1,0:T(8,128)S(1)}, u32[]{:S(2)}, u32[]{:S(2)}) collective-permute-start(f32[80,768]{1,0:T(8,128)} %get-tuple-element.75), channel_id=1, source_target_pairs={{3,0},{0,1},{1,2},{2,3},{7,4},{4,5},{5,6},{6,7},{11,8},{8,9},{9,10... | collective-permute-start | bytes 737288 | tf_op jit(solution)/shard_map/ppermute | solution.py:967
  40.8 0.7 copy-start.15
  40.8 0.8 copy-start.16
  40.8 0.8 copy-start.17
  43.8 2.4 copy-start.1
  45.9 381.1 %all-reduce.3.cloned.1.call-start = ((), (), s32[]{:S(2)}) async-start(), calls=%async_computation.1 | async-start | bytes 14254080 | tf_op jit(solution)/shard_map/psum | solution.py:1072
  46.2 17.0 %collective-permute-start.3 = (f32[3,72,768]{2,1,0:T(8,128)S(1)}, f32[3,72,768]{2,1,0:T(8,128)S(1)}, u32[]{:S(2)}, u32[]{:S(2)}) collective-permute-start(f32[3,72,768]{2,1,0:T(8,128)S(1)} %copy-done.1), channel_id=1, source_target_pairs={{0,8},{4,12},{8,0},{12,4},{16,24},{20,28},{24,16},{28,20},{1,9},{5... | collective-permute-start | bytes 1990664 | tf_op jit(solution)/shard_map/ppermute | solution.py:970
  47.8 15.5 %collective-permute-start.4 = (f32[3,72,768]{2,1,0:T(8,128)S(1)}, f32[3,72,768]{2,1,0:T(8,128)S(1)}, u32[]{:S(2)}, u32[]{:S(2)}) collective-permute-start(f32[3,72,768]{2,1,0:T(8,128)S(1)} %copy-done.1), channel_id=1, source_target_pairs={{0,16},{4,20},{8,24},{12,28},{16,0},{20,4},{24,8},{28,12},{1,17},{... | collective-permute-start | bytes 1990664 | tf_op jit(solution)/shard_map/ppermute | solution.py:970
  63.2 0.8 copy-start.2
  63.3 1.0 copy-start.3
  66.4 9.2 %collective-permute-start.5 = (f32[3,40,768]{2,1,0:T(8,128)}, f32[3,40,768]{2,1,0:T(8,128)S(1)}, u32[]{:S(2)}, u32[]{:S(2)}) collective-permute-start(f32[3,40,768]{2,1,0:T(8,128)} %get-tuple-element.89), channel_id=1, source_target_pairs={{0,16},{4,20},{8,24},{12,28},{16,0},{20,4},{24,8},{28,12},{1,17},{... | collective-permute-start | bytes 1105928 | tf_op jit(solution)/shard_map/ppermute | solution.py:970
  67.8 10.9 %collective-permute-start.7 = (f32[3,72,768]{2,1,0:T(8,128)S(1)}, f32[3,72,768]{2,1,0:T(8,128)S(1)}, u32[]{:S(2)}, u32[]{:S(2)}) collective-permute-start(f32[3,72,768]{2,1,0:T(8,128)S(1)} %copy-done.1), channel_id=1, source_target_pairs={{0,4},{4,0},{8,12},{12,8},{16,20},{20,16},{24,28},{28,24},{1,5},{5... | collective-permute-start | bytes 1990664 | tf_op jit(solution)/shard_map/ppermute | solution.py:970
  67.8 12.2 %collective-permute-start.8 = (f32[3,72,768]{2,1,0:T(8,128)}, f32[3,72,768]{2,1,0:T(8,128)S(1)}, u32[]{:S(2)}, u32[]{:S(2)}) collective-permute-start(f32[3,72,768]{2,1,0:T(8,128)} %copy-done.2), channel_id=1, source_target_pairs={{0,4},{4,0},{8,12},{12,8},{16,20},{20,16},{24,28},{28,24},{1,5},{5... | collective-permute-start | bytes 1990664 | tf_op jit(solution)/shard_map/ppermute | solution.py:970
  68.3 11.7 %collective-permute-start.9 = (f32[3,72,768]{2,1,0:T(8,128)}, f32[3,72,768]{2,1,0:T(8,128)S(1)}, u32[]{:S(2)}, u32[]{:S(2)}) collective-permute-start(f32[3,72,768]{2,1,0:T(8,128)} %copy-done.3), channel_id=1, source_target_pairs={{0,4},{4,0},{8,12},{12,8},{16,20},{20,16},{24,28},{28,24},{1,5},{5... | collective-permute-start | bytes 1990664 | tf_op jit(solution)/shard_map/ppermute | solution.py:970
  68.3 9.7 %collective-permute-start.6 = (f32[3,32,768]{2,1,0:T(8,128)}, f32[3,32,768]{2,1,0:T(8,128)}, u32[]{:S(2)}, u32[]{:S(2)}) collective-permute-start(f32[3,32,768]{2,1,0:T(8,128)} %get-tuple-element.90), channel_id=1, source_target_pairs={{0,8},{4,12},{8,0},{12,4},{16,24},{20,28},{24,16},{28,20},{1,9},{5... | collective-permute-start | bytes 884744 | tf_op jit(solution)/shard_map/ppermute | solution.py:970
  75.6 4.5 %copy-start.13 = (f32[3,40,768]{2,1,0:T(8,128)}, f32[3,40,768]{2,1,0:T(8,128)S(1)}, u32[]{:S(2)}) copy-start(f32[3,40,768]{2,1,0:T(8,128)S(1)} %collective-permute-done.5.refs_3_) | copy-start | bytes 1105924
  75.6 4.5 collective-permute-start.10
  78.1 1.9 collective-permute-start.11
  78.7 1.4 copy-start.8
  80.0 0.9 copy-start.9
  80.0 1.1 copy-start.10
  80.0 1.1 copy-start.14
  106.8 45.7 %collective-permute-start.12 = (f32[3,216,768]{2,1,0:T(8,128)}, f32[3,216,768]{2,1,0:T(8,128)}, u32[]{:S(2)}, u32[]{:S(2)}) collective-permute-start(f32[3,216,768]{2,1,0:T(8,128)} %turn_pieces.1.refs_0_.refs_2_), channel_id=1, source_target_pairs={{0,8},{4,12},{8,0},{12,4},{16,24},{20,28},{24,16},{28,20},{1,9},{5... | collective-permute-start | bytes 5971976 | tf_op jit(solution)/shard_map/ppermute | solution.py:970
  107.3 45.4 %collective-permute-start.13 = (f32[3,216,768]{2,1,0:T(8,128)}, f32[3,216,768]{2,1,0:T(8,128)}, u32[]{:S(2)}, u32[]{:S(2)}) collective-permute-start(f32[3,216,768]{2,1,0:T(8,128)} %turn_pieces.1.refs_0_.refs_2_), channel_id=1, source_target_pairs={{0,16},{4,20},{8,24},{12,28},{16,0},{20,4},{24,8},{28,12},{1,17},{... | collective-permute-start | bytes 5971976 | tf_op jit(solution)/shard_map/ppermute | solution.py:970
  145.2 13.2 %copy-start = (f32[3,216,768]{2,1,0:T(8,128)S(1)}, f32[3,216,768]{2,1,0:T(8,128)}, u32[]{:S(2)}) copy-start(f32[3,216,768]{2,1,0:T(8,128)} %turn_pieces.1.refs_0_.refs_2_) | copy-start | bytes 5971972
  156.3 24.0 %collective-permute-start.14 = (f32[3,112,768]{2,1,0:T(8,128)}, f32[3,112,768]{2,1,0:T(8,128)S(1)}, u32[]{:S(2)}, u32[]{:S(2)}) collective-permute-start(f32[3,112,768]{2,1,0:T(8,128)} %get-tuple-element.102.refs_4_), channel_id=1, source_target_pairs={{0,16},{4,20},{8,24},{12,28},{16,0},{20,4},{24,8},{28,12},{1,17},{... | collective-permute-start | bytes 3096584 | tf_op jit(solution)/shard_map/ppermute | solution.py:970
  157.1 21.9 %collective-permute-start.15 = (f32[3,104,768]{2,1,0:T(8,128)}, f32[3,104,768]{2,1,0:T(8,128)S(1)}, u32[]{:S(2)}, u32[]{:S(2)}) collective-permute-start(f32[3,104,768]{2,1,0:T(8,128)} %get-tuple-element.104), channel_id=1, source_target_pairs={{0,8},{4,12},{8,0},{12,4},{16,24},{20,28},{24,16},{28,20},{1,9},{5... | collective-permute-start | bytes 2875400 | tf_op jit(solution)/shard_map/ppermute | solution.py:970
  158.4 28.6 %collective-permute-start.16 = (f32[3,216,768]{2,1,0:T(8,128)S(1)}, f32[3,216,768]{2,1,0:T(8,128)}, u32[]{:S(2)}, u32[]{:S(2)}) collective-permute-start(f32[3,216,768]{2,1,0:T(8,128)S(1)} %copy-done), channel_id=1, source_target_pairs={{0,4},{4,0},{8,12},{12,8},{16,20},{20,16},{24,28},{28,24},{1,5},{5... | collective-permute-start | bytes 5971976 | tf_op jit(solution)/shard_map/ppermute | solution.py:970
  176.6 8.3 %copy-start.18 = (bf16[768]{0:T(1024)(128)(2,1)S(1)}, bf16[768]{0:T(1024)(128)(2,1)}, u32[]{:S(2)}) copy-start(bf16[768]{0:T(1024)(128)(2,1)} %param.30) | copy-start | bytes 4612
  176.6 8.4 %copy-start.19 = (bf16[768]{0:T(1024)(128)(2,1)S(1)}, bf16[768]{0:T(1024)(128)(2,1)}, u32[]{:S(2)}) copy-start(bf16[768]{0:T(1024)(128)(2,1)} %param.31) | copy-start | bytes 4612
  176.6 8.6 %copy-start.20 = (bf16[768]{0:T(1024)(128)(2,1)S(1)}, bf16[768]{0:T(1024)(128)(2,1)}, u32[]{:S(2)}) copy-start(bf16[768]{0:T(1024)(128)(2,1)} %param.32) | copy-start | bytes 4612
  176.6 8.8 %copy-start.21 = (bf16[768]{0:T(1024)(128)(2,1)S(1)}, bf16[768]{0:T(1024)(128)(2,1)}, u32[]{:S(2)}) copy-start(bf16[768]{0:T(1024)(128)(2,1)} %param.36) | copy-start | bytes 4612
  176.6 9.0 %copy-start.22 = (bf16[768]{0:T(1024)(128)(2,1)S(1)}, bf16[768]{0:T(1024)(128)(2,1)}, u32[]{:S(2)}) copy-start(bf16[768]{0:T(1024)(128)(2,1)} %param.37) | copy-start | bytes 4612
  176.6 9.2 %copy-start.23 = (bf16[768]{0:T(1024)(128)(2,1)S(1)}, bf16[768]{0:T(1024)(128)(2,1)}, u32[]{:S(2)}) copy-start(bf16[768]{0:T(1024)(128)(2,1)} %param.38) | copy-start | bytes 4612
  176.6 10.3 %collective-permute-start.17 = (f32[3,216,768]{2,1,0:T(8,128)}, f32[3,216,768]{2,1,0:T(8,128)}, u32[]{:S(2)}, u32[]{:S(2)}) collective-permute-start(f32[3,216,768]{2,1,0:T(8,128)} %collective-permute-done.12.side.refs_3_), channel_id=1, source_target_pairs={{0,4},{4,0},{8,12},{12,8},{16,20},{20,16},{24,28},{28,24},{1,5},{5... | collective-permute-start | bytes 5971976 | tf_op jit(solution)/shard_map/ppermute | solution.py:970
  177.2 9.8 %collective-permute-start.18 = (f32[3,216,768]{2,1,0:T(8,128)}, f32[3,216,768]{2,1,0:T(8,128)}, u32[]{:S(2)}, u32[]{:S(2)}) collective-permute-start(f32[3,216,768]{2,1,0:T(8,128)} %collective-permute-done.13.ahead.refs_4_), channel_id=1, source_target_pairs={{0,4},{4,0},{8,12},{12,8},{16,20},{20,16},{24,28},{28,24},{1,5},{5... | collective-permute-start | bytes 5971976 | tf_op jit(solution)/shard_map/ppermute | solution.py:970
  178.9 1.3 copy-start.7
  180.3 1.0 copy-start.6
  184.2 4.3 collective-permute-start.19
  427.0 7.2 %copy-start.12 = (f32[768,192]{0,1:T(8,128)S(1)}, f32[768,192]{0,1:T(8,128)}, u32[]{:S(2)}) copy-start(f32[768,192]{0,1:T(8,128)} %get-tuple-element.154) | copy-start | bytes 1769476
  427.0 8.0 %copy-start.11 = (f32[768,192]{0,1:T(8,128)S(1)}, f32[768,192]{0,1:T(8,128)}, u32[]{:S(2)}) copy-start(f32[768,192]{0,1:T(8,128)} %get-tuple-element.156) | copy-start | bytes 1769476
  427.0 8.8 %copy-start.5 = (f32[768,768]{1,0:T(8,128)S(1)}, f32[768,768]{1,0:T(8,128)}, u32[]{:S(2)}) copy-start(f32[768,768]{1,0:T(8,128)} %get-tuple-element.162) | copy-start | bytes 7077892
  435.8 2.5 copy-start.4
Sparse Core Ops, SparseCore 0:
  46.0 55.8 all-gather.2
  312.6 114.3 all-reduce.2
